TPU v7x, 32 devices: a whole 2x2x4 slice. The times are simulated.
32 devices in a mesh: seq: 8 (over z, y), fsdp: 4 (over x, core).
Axes of the slice: x: 2, y: 2, z: 4, core: 2. Of those that a mesh axis runs over, the one named last changes fastest.
Arguments:
- tokens_in: bfloat16 [2, 2048, 2048], P(None, 'seq', 'fsdp'), may hold values from -6 to 6
- cotangent: bfloat16 [2, 2048, 2048], P(None, 'seq', 'fsdp'), may hold values from -6 to 6
- gain_attn: bfloat16 [2048], P('seq'), may hold values from 0.099609375 to 1.8984375
- query_weight: bfloat16 [2048, 2048], P('seq', 'fsdp'), may hold values from -0.0625 to 0.0625
- key_weight: bfloat16 [2048, 2048], P('seq', 'fsdp'), may hold values from -0.0625 to 0.0625
- value_weight: bfloat16 [2048, 2048], P('seq', 'fsdp'), may hold values from -0.125 to 0.125
- output_weight: bfloat16 [2048, 2048], P('seq', 'fsdp'), may hold values from -0.75 to 0.75
- bias_table: bfloat16 [32, 32], P('seq', 'fsdp'), may hold values from -6 to 6
- gain_ffn: bfloat16 [2048], P('seq'), may hold values from 0.099609375 to 1.8984375
- gate_weight: bfloat16 [2048, 5120], P('seq', 'fsdp'), may hold values from -0.125 to 0.125
- up_weight: bfloat16 [2048, 5120], P('seq', 'fsdp'), may hold values from -0.125 to 0.125
- down_weight: bfloat16 [2048, 5120], P('seq', 'fsdp'), may hold values from -0.078125 to 0.078125
- lengths: int32 [2], replicated, may hold values from 256 to 2048, as said below
- buckets: int32 [4095], replicated, may hold values from 0 to 31
Outputs:
- layer_out: bfloat16 [2, 2048, 2048], P(None, 'seq', 'fsdp')
- grad_tokens: float32 [2, 2048, 2048], P(None, 'seq', 'fsdp')
- grad_gain_attn: float32 [2048], P('seq')
- grad_query: float32 [2048, 2048], P('seq', 'fsdp')
- grad_key: float32 [2048, 2048], P('seq', 'fsdp')
- grad_value: float32 [2048, 2048], P('seq', 'fsdp')
- grad_output: float32 [2048, 2048], P('seq', 'fsdp')
- grad_table: float32 [32, 32], P('seq', 'fsdp')
- grad_gain_ffn: float32 [2048], P('seq')
- grad_gate: float32 [2048, 5120], P('seq', 'fsdp')
- grad_up: float32 [2048, 5120], P('seq', 'fsdp')
- grad_down: float32 [2048, 5120], P('seq', 'fsdp')
Inputs may be any that keep to these rules, and one draw needn't show every extreme that they name: `lengths`: exactly one of the 2 sequences is valid over all 2048 slots; the others end at least 256 slots earlier.
All inputs are finite; a program needn't handle non-finite values.
Results may differ from a plain program's by a relative error of at most 0.014.
The roundings to bfloat16 on the way count: a program that leaves them out, or rounds other values in their place, can miss the bound.
Values may be sent and summed in bfloat16 or wider, within the bound.
A program may use at most 384 MiB of HBM per device.

v0:
```python
from functools import partial

import jax
import jax.numpy as jnp
from jax import lax
from jax.sharding import PartitionSpec as P

DH = 64


epsilon = 1e-06
highest = lax.Precision.HIGHEST
masked_score = -1e30


def plain_product(left, right):
    return jnp.dot(left, right, preferred_element_type=jnp.float32)


def right_transposed(left, right):
    return lax.dot_general(
        left, right, (((1,), (1,)), ((), ())), preferred_element_type=jnp.float32
    )


def left_transposed(left, right):
    return lax.dot_general(
        left, right, (((0,), (0,)), ((), ())), preferred_element_type=jnp.float32
    )


def normalize(rows, gain):
    row_scale = lax.rsqrt(jnp.mean(rows * rows, axis=-1, keepdims=True) + epsilon)
    unit_rows = rows * row_scale
    return (unit_rows, row_scale, (unit_rows * gain.astype(jnp.float32)).astype(jnp.bfloat16))


def norm_back(grad_normed, unit_rows, row_scale, gain):
    weighted = grad_normed * gain.astype(jnp.float32)
    return row_scale * (
        weighted - unit_rows * jnp.mean(weighted * unit_rows, axis=-1, keepdims=True)
    )


def to_heads(rows, batch_count, head_size):
    slot_count = rows.shape[0] // batch_count
    number_of_heads = rows.shape[1] // head_size
    return rows.reshape(batch_count, slot_count, number_of_heads, head_size).transpose(2, 0, 1, 3)


def from_heads(blocks):
    number_of_heads, batch_count, slot_count, head_size = blocks.shape
    return blocks.transpose(1, 2, 0, 3).reshape(
        batch_count * slot_count, number_of_heads * head_size
    )


def bias_rows(bias_line, first_query, slot_count, length):
    span = slot_count + length - 1
    segment = lax.dynamic_slice_in_dim(bias_line, length - first_query - slot_count, span)
    flat = jnp.tile(segment, slot_count)
    skewed = flat[slot_count - 1 : slot_count - 1 + slot_count * (span - 1)].reshape(
        slot_count, span - 1
    )
    return skewed[:, :length]


def bias_rows_back(block_grad, first_query, slot_count, length, line_length):
    span = slot_count + length - 1
    widened = jnp.pad(block_grad, ((0, 0), (0, span - 1 - length)))
    flat = jnp.pad(widened.reshape(-1), (slot_count - 1, 1))
    segment_grad = jnp.sum(flat.reshape(slot_count, span), axis=0)
    return lax.dynamic_update_slice_in_dim(
        jnp.zeros((line_length,), jnp.float32), segment_grad, length - first_query - slot_count, 0
    )


def full_features(block):
    gathered = lax.all_gather(block, "fsdp", axis=2, tiled=True)
    return gathered.reshape(gathered.shape[0] * gathered.shape[1], gathered.shape[2])


def feature_total(partial_rows):
    return lax.psum(partial_rows, "fsdp")


def shards(
    tokens_in,
    cotangent,
    gain_attn,
    query_weight,
    key_weight,
    value_weight,
    output_weight,
    bias_table,
    gain_ffn,
    gate_weight,
    up_weight,
    down_weight,
    lengths,
    buckets,
):
    batch_count, slot_count, part_width = tokens_in.shape
    head_size = DH
    seq_index = lax.axis_index("seq")
    fsdp_index = lax.axis_index("fsdp")
    length = slot_count * lax.axis_size("seq")
    line_length = buckets.shape[0]
    first_query = seq_index * slot_count
    positions = jnp.arange(length, dtype=jnp.int32)
    query_positions = first_query + jnp.arange(slot_count, dtype=jnp.int32)
    key_valid = positions[None, :] < lengths[:, None]
    own_valid = query_positions[None, :] < lengths[:, None]
    gain_one, query_full, key_full, value_full, output_full, table_full = (
        lax.all_gather(gain_attn, "seq", axis=0, tiled=True),
        lax.all_gather(query_weight, "seq", axis=0, tiled=True),
        lax.all_gather(key_weight, "seq", axis=0, tiled=True),
        lax.all_gather(value_weight, "seq", axis=0, tiled=True),
        lax.all_gather(output_weight, "seq", axis=0, tiled=True),
        lax.all_gather(bias_table, "seq", axis=0, tiled=True),
    )
    token_rows = full_features(tokens_in).astype(jnp.float32)
    unit_one, scale_one, normed_one = normalize(token_rows, gain_one)
    query_heads = to_heads(
        plain_product(normed_one, query_full).astype(jnp.bfloat16), batch_count, head_size
    )
    key_heads = to_heads(
        plain_product(normed_one, key_full).astype(jnp.bfloat16), batch_count, head_size
    )
    value_heads = to_heads(
        plain_product(normed_one, value_full).astype(jnp.bfloat16), batch_count, head_size
    )
    number_of_heads = query_heads.shape[0]
    flat_shape = (number_of_heads, batch_count, slot_count * head_size)
    gathered_keys, gathered_values = (
        lax.all_gather(key_heads.reshape(flat_shape), "seq", axis=2, tiled=True),
        lax.all_gather(value_heads.reshape(flat_shape), "seq", axis=2, tiled=True),
    )
    all_keys = gathered_keys.reshape(number_of_heads, batch_count, length, head_size)
    all_values = gathered_values.reshape(number_of_heads, batch_count, length, head_size)
    bucket_hot = (
        buckets[:, None] == jnp.arange(table_full.shape[0], dtype=jnp.int32)[None, :]
    ).astype(jnp.float32)
    offset_bias = lax.dot_general(
        table_full.astype(jnp.float32), bucket_hot, (((0,), (1,)), ((), ())), precision=highest
    )

    def masked_scores(query_tile_rows, key_tile_rows, bias_block):
        raw = (
            jnp.einsum(
                "jht,jxt->jhx", query_tile_rows, key_tile_rows, preferred_element_type=jnp.float32
            )
            + bias_block[None]
        )
        return jnp.where(key_valid[:, None, :], raw, masked_score)

    def attend(inputs):
        query_tile_rows, key_tile_rows, value_tile_rows, bias_line = inputs
        scores = masked_scores(
            query_tile_rows, key_tile_rows, bias_rows(bias_line, first_query, slot_count, length)
        )
        row_peak = jnp.max(scores, axis=-1, keepdims=True)
        raised = jnp.exp(scores - row_peak)
        denominator = jnp.sum(raised, axis=-1, keepdims=True)
        weights_reduced_precision = (raised / denominator).astype(jnp.bfloat16)
        context = jnp.einsum(
            "wot,wtf->wof",
            weights_reduced_precision,
            value_tile_rows,
            preferred_element_type=jnp.float32,
        ).astype(jnp.bfloat16)
        return (context, (row_peak + jnp.log(denominator))[..., 0])

    context_heads, log_totals = lax.map(attend, (query_heads, all_keys, all_values, offset_bias))
    context_rows = from_heads(context_heads)
    residual = token_rows + feature_total(right_transposed(context_rows, output_full))
    gain_two, gate_full, up_full, down_full = (
        lax.all_gather(gain_ffn, "seq", axis=0, tiled=True),
        lax.all_gather(gate_weight, "seq", axis=0, tiled=True),
        lax.all_gather(up_weight, "seq", axis=0, tiled=True),
        lax.all_gather(down_weight, "seq", axis=0, tiled=True),
    )
    unit_two, scale_two, normed_two = normalize(residual, gain_two)
    gate_pre = plain_product(normed_two, gate_full)
    up_pre = plain_product(normed_two, up_full)
    activated, gelu_back = jax.vjp(jax.nn.gelu, gate_pre)
    hidden = (activated * up_pre).astype(jnp.bfloat16)
    ffn_share = lax.psum_scatter(
        right_transposed(hidden, down_full), "fsdp", scatter_dimension=1, tiled=True
    )
    residual_share = lax.dynamic_slice_in_dim(residual, fsdp_index * part_width, part_width, 1)
    layer_out = (
        (residual_share + ffn_share)
        .astype(jnp.bfloat16)
        .reshape(batch_count, slot_count, part_width)
    )
    masked_cot = jnp.where(own_valid[:, :, None], cotangent, jnp.zeros_like(cotangent))
    grad_rows = full_features(masked_cot)
    grad_down = left_transposed(grad_rows, hidden)
    grad_hidden = plain_product(grad_rows, down_full)
    grad_gate_pre = gelu_back(grad_hidden * up_pre)[0].astype(jnp.bfloat16)
    grad_up_pre = (grad_hidden * activated).astype(jnp.bfloat16)
    grad_gate = left_transposed(normed_two, grad_gate_pre)
    grad_up = left_transposed(normed_two, grad_up_pre)
    normed_two_grad = right_transposed(grad_gate_pre, gate_full) + right_transposed(
        grad_up_pre, up_full
    )
    second_gain_piece = jnp.sum(normed_two_grad * unit_two, axis=0)
    ffn_grads = (
        lax.psum_scatter(second_gain_piece, "seq", scatter_dimension=0, tiled=True),
        lax.psum_scatter(grad_gate, "seq", scatter_dimension=0, tiled=True),
        lax.psum_scatter(grad_up, "seq", scatter_dimension=0, tiled=True),
        lax.psum_scatter(grad_down, "seq", scatter_dimension=0, tiled=True),
    )
    residual_grad = grad_rows.astype(jnp.float32) + norm_back(
        feature_total(normed_two_grad), unit_two, scale_two, gain_two
    )
    residual_low = residual_grad.astype(jnp.bfloat16)
    grad_output = left_transposed(residual_low, context_rows)
    context_grad = to_heads(
        plain_product(residual_low, output_full).astype(jnp.bfloat16), batch_count, head_size
    )

    def query_side(inputs, with_keys):
        query_tile_rows, key_tile_rows, value_tile_rows, bias_line, log_total, context_tile_rows = (
            inputs
        )
        scores = masked_scores(
            query_tile_rows, key_tile_rows, bias_rows(bias_line, first_query, slot_count, length)
        )
        probs = jnp.exp(scores - log_total[..., None])
        prob_grad = jnp.einsum(
            "jht,jxt->jhx", context_tile_rows, value_tile_rows, preferred_element_type=jnp.float32
        )
        delta = jnp.sum(probs * prob_grad, axis=-1)
        score_gradient = (probs * (prob_grad - delta[..., None])).astype(jnp.bfloat16)
        query_grad = jnp.einsum(
            "wot,wtf->wof", score_gradient, key_tile_rows, preferred_element_type=jnp.float32
        )
        bias_grad = bias_rows_back(
            jnp.sum(score_gradient.astype(jnp.float32), axis=0),
            first_query,
            slot_count,
            length,
            line_length,
        )
        key_term = jnp.einsum(
            "xic,xil->xcl", score_gradient, query_tile_rows, preferred_element_type=jnp.float32
        )
        value_term = jnp.einsum(
            "xic,xil->xcl",
            probs.astype(jnp.bfloat16),
            context_tile_rows,
            preferred_element_type=jnp.float32,
        )
        return (query_grad, bias_grad, delta, key_term, value_term)

    side_inputs = (query_heads, all_keys, all_values, offset_bias, log_totals, context_grad)
    query_grad, bias_grad, delta, key_terms, value_terms = lax.map(
        partial(query_side, with_keys=True), side_inputs
    )
    wide_shape = (number_of_heads, batch_count, length * head_size)
    key_sums, value_sums = (
        lax.psum_scatter(key_terms.reshape(wide_shape), "seq", scatter_dimension=2, tiled=True),
        lax.psum_scatter(value_terms.reshape(wide_shape), "seq", scatter_dimension=2, tiled=True),
    )
    own_shape = (number_of_heads, batch_count, slot_count, head_size)
    query_low = from_heads(query_grad.astype(jnp.bfloat16))
    key_low = from_heads(key_sums.reshape(own_shape).astype(jnp.bfloat16))
    value_low = from_heads(value_sums.reshape(own_shape).astype(jnp.bfloat16))
    grad_query = left_transposed(normed_one, query_low)
    grad_key = left_transposed(normed_one, key_low)
    grad_value = left_transposed(normed_one, value_low)
    grad_table = lax.dot_general(bucket_hot, bias_grad, (((0,), (1,)), ((), ())), precision=highest)
    normed_one_grad = (
        right_transposed(query_low, query_full)
        + right_transposed(key_low, key_full)
        + right_transposed(value_low, value_full)
    )
    gain_one_part = jnp.sum(normed_one_grad * unit_one, axis=0)
    attn_grads = (
        lax.psum_scatter(gain_one_part, "seq", scatter_dimension=0, tiled=True),
        lax.psum_scatter(grad_query, "seq", scatter_dimension=0, tiled=True),
        lax.psum_scatter(grad_key, "seq", scatter_dimension=0, tiled=True),
        lax.psum_scatter(grad_value, "seq", scatter_dimension=0, tiled=True),
        lax.psum_scatter(grad_output, "seq", scatter_dimension=0, tiled=True),
        lax.psum_scatter(grad_table, "seq", scatter_dimension=0, tiled=True),
    )
    token_grad = residual_grad + norm_back(
        feature_total(normed_one_grad), unit_one, scale_one, gain_one
    )
    token_share = lax.dynamic_slice_in_dim(
        token_grad, fsdp_index * part_width, part_width, 1
    ).reshape(batch_count, slot_count, part_width)
    gain_one_sum, gain_two_sum = lax.psum((attn_grads[0], ffn_grads[0]), "fsdp")
    return (
        layer_out,
        token_share,
        gain_one_sum,
        attn_grads[1],
        attn_grads[2],
        attn_grads[3],
        attn_grads[4],
        attn_grads[5],
        gain_two_sum,
        ffn_grads[1],
        ffn_grads[2],
        ffn_grads[3],
    )


def solution(mesh):
    placed = (
        P(None, "seq", "fsdp"),
        P(None, "seq", "fsdp"),
        P("seq"),
        P("seq", "fsdp"),
        P("seq", "fsdp"),
        P("seq", "fsdp"),
        P("seq", "fsdp"),
        P("seq", "fsdp"),
        P("seq"),
        P("seq", "fsdp"),
        P("seq", "fsdp"),
        P("seq", "fsdp"),
        P(),
        P(),
    )
    return jax.shard_map(
        shards,
        mesh=mesh,
        in_specs=placed,
        out_specs=(
            P(None, "seq", "fsdp"),
            P(None, "seq", "fsdp"),
            P("seq"),
            P("seq", "fsdp"),
            P("seq", "fsdp"),
            P("seq", "fsdp"),
            P("seq", "fsdp"),
            P("seq", "fsdp"),
            P("seq"),
            P("seq", "fsdp"),
            P("seq", "fsdp"),
            P("seq", "fsdp"),
        ),
        check_vma=False,
    )
```

profile of v0, /device:TPU:0, one launch (start us, length us, event | category | flops | bytes accessed | tf_op | source)
XLA Modules:
  0.0 2738.2 jit_solution(14807744632918372417)
XLA Ops:
  10.7 22.3 all-gather
  42.3 44.1 %all-gather.19.cloned.1.call-done = bf16[2048,512]{1,0:T(8,128)(2,1)} async-done(((bf16[256,512]{1,0:T(8,128)(2,1)}), bf16[2048,512]{1,0:T(8,128)(2,1)}) %all-gather.19.cloned.1.call-update) | async-done | bytes 2097168 | tf_op jit(solution)/shard_map/all_gather | solution.py:117
  91.9 44.4 %all-gather.23.cloned.1.call-done = bf16[2048,512]{1,0:T(8,128)(2,1)} async-done(((bf16[256,512]{1,0:T(8,128)(2,1)}), bf16[2048,512]{1,0:T(8,128)(2,1)}) %all-gather.23.cloned.1.call-update) | async-done | bytes 2097168 | tf_op jit(solution)/shard_map/all_gather | solution.py:118
  143.3 18.3 all-gather.1
  162.5 23.6 all-gather.17.cloned.1.call-done
  190.0 70.6 %all-gather.21.cloned.1.call-done = bf16[8,2,131072]{2,0,1:T(8,128)(2,1)} async-done(((bf16[8,2,16384]{2,0,1:T(8,128)(2,1)}), bf16[8,2,131072]{2,0,1:T(8,128)(2,1)}) %all-gather.21.cloned.1.call-update) | async-done | bytes 4194320 | tf_op jit(solution)/shard_map/all_gather | solution.py:136
  260.6 11.3 reshape.258
  271.9 8.6 copy.72
  280.5 54.4 %all-gather.25.cloned.1.call-done = bf16[8,2,131072]{2,0,1:T(8,128)(2,1)} async-done(((bf16[8,2,16384]{2,0,1:T(8,128)(2,1)}), bf16[8,2,131072]{2,0,1:T(8,128)(2,1)}) %all-gather.25.cloned.1.call-update) | async-done | bytes 4194320 | tf_op jit(solution)/shard_map/all_gather | solution.py:137
  334.9 11.3 reshape.261
  346.2 8.5 copy.73
  354.7 131.9 %while.36 = (s32[]{:T(128)}, bf16[8,2,256,64]{2,3,1,0:T(8,128)(2,1)S(1)}, f32[8,2,256]{2,1,0:T(2,128)S(1)}, bf16[8,2,256,64]{2,3,1,0:T(8,128)(2,1)S(1)}, bf16[8,...) while((s32[]{:T(128)}, ...), condition=%wide.region_4.5_spmd.clone, body=%wide.region_1.4_spmd.clone.sunk | while | flops 281054720 | bytes 40822932 | solution.py:174
  496.0 18.2 all-gather.2
  514.1 62.8 %all-reduce.11.cloned.1.call-done = f32[512,2048]{1,0:T(8,128)} async-done(((f32[512,2048]{1,0:T(8,128)}), f32[512,2048]{1,0:T(8,128)}) %all-reduce.11.cloned.1.call-update) | async-done | bytes 4194320 | tf_op jit(solution)/shard_map/psum | solution.py:84
  582.2 83.6 %all-gather.29.cloned.1.call-done = bf16[2048,1280]{1,0:T(8,128)(2,1)} async-done(((bf16[256,1280]{1,0:T(8,128)(2,1)}), bf16[2048,1280]{1,0:T(8,128)(2,1)}) %all-gather.29.cloned.1.call-update) | async-done | bytes 5242896 | tf_op jit(solution)/shard_map/all_gather | solution.py:179
  665.8 6.8 fusion.58
  672.6 79.9 %all-gather.31.cloned.1.call-done = bf16[2048,1280]{1,0:T(8,128)(2,1)} async-done(((bf16[256,1280]{1,0:T(8,128)(2,1)}), bf16[2048,1280]{1,0:T(8,128)(2,1)}) %all-gather.31.cloned.1.call-update) | async-done | bytes 5242896 | tf_op jit(solution)/shard_map/all_gather | solution.py:180
  752.5 6.8 fusion.59
  759.3 16.2 all-gather.35.cloned.1.call-done
  775.6 88.6 %all-gather.33.cloned.1.call-done = bf16[2048,1280]{1,0:T(8,128)(2,1)} async-done(((bf16[256,1280]{1,0:T(8,128)(2,1)}), bf16[2048,1280]{1,0:T(8,128)(2,1)}) %all-gather.33.cloned.1.call-update) | async-done | bytes 5242896 | tf_op jit(solution)/shard_map/all_gather | solution.py:181
  864.1 10.2 multiply_convert_fusion.3
  874.3 5.9 fusion.61
  884.9 83.7 %all-reduce.13.cloned.1.call-done = f32[512,2048]{1,0:T(8,128)} async-done(((f32[512,2048]{1,0:T(8,128)}), f32[512,2048]{1,0:T(8,128)}) %all-reduce.13.cloned.1.call-update) | async-done | bytes 4194320 | tf_op jit(solution)/shard_map/psum | solution.py:84
  968.6 6.4 multiply_reduce_fusion.1
  980.4 374.9 %while.37 = (s32[]{:T(128)}, bf16[8,2,256,64]{2,3,1,0:T(8,128)(2,1)}, f32[8,4095]{1,0:T(8,128)}, f32[8,2,2048,64]{2,3,1,0:T(8,128)}, f32[8,2,2048,64]{2,3,1,0:T(...) while((s32[]{:T(128)}, ...), condition=%wide.region_14.15_spmd.clone, body=%wide.region_10.14_spmd.clone.sunk | while | flops 682689536 | bytes 115206392 | solution.py:259
  1013.9 4.9 reshape.297
  1355.3 12.2 copy.81
  1367.5 15.5 reshape.267
  1383.0 12.2 copy.83
  1395.3 15.5 reshape.269
  1412.1 6.9 fusion.60
  1424.3 107.9 %reduce-scatter.13.cloned.1.call-done = f32[8,2,16384]{2,0,1:T(8,128)} async-done(((f32[8,2,131072]{2,0,1:T(8,128)}), f32[8,2,16384]{2,0,1:T(8,128)}) %reduce-scatter.13.cloned.1.call-update) | async-done | bytes 1048592 | tf_op jit(solution)/shard_map/reduce_scatter | solution.py:264
  1535.5 148.7 %reduce-scatter.15.cloned.1.call-done = f32[8,2,16384]{2,0,1:T(8,128)} async-done(((f32[8,2,131072]{2,0,1:T(8,128)}), f32[8,2,16384]{2,0,1:T(8,128)}) %reduce-scatter.15.cloned.1.call-update) | async-done | bytes 1048592 | tf_op jit(solution)/shard_map/reduce_scatter | solution.py:265
  1702.1 5.6 fusion.50
  1707.7 8.9 fusion.67
  1717.0 8.7 fusion.68
  1725.8 8.8 fusion.69
  1747.9 70.1 %all-reduce.15.cloned.1.call-done = f32[512,2048]{1,0:T(8,128)} async-done(((f32[512,2048]{1,0:T(8,128)}), f32[512,2048]{1,0:T(8,128)}) %all-reduce.15.cloned.1.call-update) | async-done | bytes 4194320 | tf_op jit(solution)/shard_map/psum | solution.py:84
  1818.0 6.5 multiply_reduce_fusion.2
  1824.4 38.6 %all-reduce.5 = (f32[2048]{0:T(1024)S(1)}, f32[32,8]{1,0:T(8,128)S(1)}, f32[2048]{0:T(1024)S(1)}) all-reduce(f32[2048]{0:T(1024)S(1)} %get-tuple-element.532, f32[32,8]{1,0:T(8,128)S(1)} %fusion.53, f32[2048]{0:T(1024)S(1)} %copy-done.25), channel_id=5, replica_groups=mesh['seq'=8,'fsdp'=4] {'seq'}, use_global_device_ids=true, to_apply=%region_20.21.clone | all-reduce | flops 4352 | bytes 34816
  1863.2 6.6 all-reduce.6
  1873.4 37.4 %reduce-scatter.17.cloned.1.call-done = f32[256,512]{1,0:T(8,128)} async-done(((f32[2048,512]{1,0:T(8,128)}), f32[256,512]{1,0:T(8,128)}) %reduce-scatter.17.cloned.1.call-update) | async-done | bytes 524304 | tf_op jit(solution)/shard_map/reduce_scatter | solution.py:283
  1910.8 92.3 %reduce-scatter.23.cloned.1.call-done = f32[256,512]{1,0:T(8,128)} async-done(((f32[2048,512]{1,0:T(8,128)}), f32[256,512]{1,0:T(8,128)}) %reduce-scatter.23.cloned.1.call-update) | async-done | bytes 524304 | tf_op jit(solution)/shard_map/reduce_scatter | solution.py:286
  2003.2 181.7 %reduce-scatter.25.cloned.1.call-done = f32[256,1280]{1,0:T(8,128)} async-done(((f32[2048,1280]{1,0:T(8,128)}), f32[256,1280]{1,0:T(8,128)}) %reduce-scatter.25.cloned.1.call-update) | async-done | bytes 1310736 | tf_op jit(solution)/shard_map/reduce_scatter | solution.py:211
  2184.9 181.2 %reduce-scatter.27.cloned.1.call-done = f32[256,1280]{1,0:T(8,128)} async-done(((f32[2048,1280]{1,0:T(8,128)}), f32[256,1280]{1,0:T(8,128)}) %reduce-scatter.27.cloned.1.call-update) | async-done | bytes 1310736 | tf_op jit(solution)/shard_map/reduce_scatter | solution.py:212
  2366.1 181.2 %reduce-scatter.29.cloned.1.call-done = f32[256,1280]{1,0:T(8,128)} async-done(((f32[2048,1280]{1,0:T(8,128)}), f32[256,1280]{1,0:T(8,128)}) %reduce-scatter.29.cloned.1.call-update) | async-done | bytes 1310736 | tf_op jit(solution)/shard_map/reduce_scatter | solution.py:213
  2547.3 91.4 %reduce-scatter.19.cloned.1.call-done = f32[256,512]{1,0:T(8,128)} async-done(((f32[2048,512]{1,0:T(8,128)}), f32[256,512]{1,0:T(8,128)}) %reduce-scatter.19.cloned.1.call-update) | async-done | bytes 524304 | tf_op jit(solution)/shard_map/reduce_scatter | solution.py:284
  2638.7 92.2 %reduce-scatter.21.cloned.1.call-done = f32[256,512]{1,0:T(8,128)} async-done(((f32[2048,512]{1,0:T(8,128)}), f32[256,512]{1,0:T(8,128)}) %reduce-scatter.21.cloned.1.call-update) | async-done | bytes 524304 | tf_op jit(solution)/shard_map/reduce_scatter | solution.py:285
  (501 shorter events, 598.0 us)
Async XLA Ops:
  7.2 27.7 %all-gather.15.cloned.1.call-start = ((), (), s32[]{:S(2)}) async-start(), calls=%async_computation.10 | async-start | bytes 2621440 | tf_op jit(solution)/shard_map/all_gather | solution.py:79
  7.9 78.4 %all-gather.19.cloned.1.call-start = ((), (), s32[]{:S(2)}) async-start(), calls=%async_computation.12 | async-start | bytes 2359296 | tf_op jit(solution)/shard_map/all_gather | solution.py:117
  8.7 127.6 %all-gather.23.cloned.1.call-start = ((), (), s32[]{:S(2)}) async-start(), calls=%async_computation.14 | async-start | bytes 2359296 | tf_op jit(solution)/shard_map/all_gather | solution.py:118
  9.4 176.7 %all-gather.17.cloned.1.call-start = ((), (), s32[]{:S(2)}) async-start(), calls=%async_computation.11 | async-start | bytes 2359296 | tf_op jit(solution)/shard_map/all_gather | solution.py:116
  10.0 250.6 %all-gather.21.cloned.1.call-start = ((), (), s32[]{:S(2)}) async-start(), calls=%async_computation.13 | async-start | bytes 4718592 | tf_op jit(solution)/shard_map/all_gather | solution.py:136
  32.9 9.3 copy-start.20
  42.3 44.1 %copy-start.16 = (bf16[512,2048]{1,0:T(8,128)(2,1)}, bf16[512,2048]{1,0:T(8,128)(2,1)S(1)}, u32[]{:S(2)}) copy-start(bf16[512,2048]{1,0:T(8,128)(2,1)S(1)} %get-tuple-element.598) | copy-start | bytes 6291460
  91.9 243.0 %all-gather.25.cloned.1.call-start = ((), (), s32[]{:S(2)}) async-start(), calls=%async_computation.15 | async-start | bytes 4718592 | tf_op jit(solution)/shard_map/all_gather | solution.py:137
  139.8 3.5 copy-start.29
  139.8 21.8 copy-start.26
  142.4 344.8 %all-gather.27.cloned.1.call-start = ((), (), s32[]{:S(2)}) async-start(), calls=%async_computation.16 | async-start | bytes 2359296 | tf_op jit(solution)/shard_map/all_gather | solution.py:119
  143.2 433.7 %all-reduce.11.cloned.1.call-start = ((), (), s32[]{:S(2)}) async-start(), calls=%async_computation.17 | async-start | bytes 8388608 | tf_op jit(solution)/shard_map/psum | solution.py:84
  346.2 8.5 copy-start.22
  492.9 3.1 copy-start.32
  492.9 84.1 %copy-start.4 = (bf16[2,256,2048]{2,1,0:T(8,128)(2,1)S(1)}, bf16[2,256,2048]{2,1,0:T(8,128)(2,1)}, u32[]{:S(2)}) copy-start(bf16[2,256,2048]{2,1,0:T(8,128)(2,1)} %all-gather.15.cloned.1.call-done) | copy-start | bytes 6291460
  492.9 172.9 %all-gather.29.cloned.1.call-start = ((), (), s32[]{:S(2)}) async-start(), calls=%async_computation.18 | async-start | bytes 5898240 | tf_op jit(solution)/shard_map/all_gather | solution.py:179
  493.6 258.9 %all-gather.31.cloned.1.call-start = ((), (), s32[]{:S(2)}) async-start(), calls=%async_computation.19 | async-start | bytes 5898240 | tf_op jit(solution)/shard_map/all_gather | solution.py:180
  494.2 281.3 %all-gather.35.cloned.1.call-start = ((), (), s32[]{:S(2)}) async-start(), calls=%async_computation.22 | async-start | bytes 2621440 | tf_op jit(solution)/shard_map/all_gather | solution.py:79
  495.3 368.8 %all-gather.33.cloned.1.call-start = ((), (), s32[]{:S(2)}) async-start(), calls=%async_computation.20 | async-start | bytes 5898240 | tf_op jit(solution)/shard_map/all_gather | solution.py:181
  495.9 472.7 %all-reduce.13.cloned.1.call-start = ((), (), s32[]{:S(2)}) async-start(), calls=%async_computation.23 | async-start | bytes 8388608 | tf_op jit(solution)/shard_map/psum | solution.py:84
  582.2 170.3 %copy-start.13 = (bf16[512,2048]{1,0:T(8,128)(2,1)}, bf16[512,2048]{1,0:T(8,128)(2,1)S(1)}, u32[]{:S(2)}) copy-start(bf16[512,2048]{1,0:T(8,128)(2,1)S(1)} %multiply_convert_fusion.1) | copy-start | bytes 6291460
  874.3 5.9 copy-start.36
  874.3 5.9 copy-start.35
  874.3 5.9 copy-start.30
  884.8 647.4 %reduce-scatter.13.cloned.1.call-start = ((), (), s32[]{:S(2)}) async-start(), calls=%async_computation.24 | async-start | bytes 9437184 | tf_op jit(solution)/shard_map/reduce_scatter | solution.py:264
  884.9 90.1 %copy-start.18 = (bf16[2,256,2048]{2,1,0:T(8,128)(2,1)S(1)}, bf16[2,256,2048]{2,1,0:T(8,128)(2,1)}, u32[]{:S(2)}) copy-start(bf16[2,256,2048]{2,1,0:T(8,128)(2,1)} %all-gather.35.cloned.1.call-done) | copy-start | bytes 6291460
  968.6 6.4 copy-start.3
  968.6 7.1 copy-start.8
  975.7 3.0 copy-start.15
  994.0 2.8 copy-start.1
  1040.8 2.8 copy-start.1
  1087.5 2.8 copy-start.1
  1383.0 301.2 %reduce-scatter.15.cloned.1.call-start = ((), (), s32[]{:S(2)}) async-start(), calls=%async_computation.25 | async-start | bytes 9437184 | tf_op jit(solution)/shard_map/reduce_scatter | solution.py:265
  1410.8 334.6 %reduce-scatter.11.cloned.1.call-start = ((), (), s32[]{:S(2)}) async-start(), calls=%async_computation.21 | async-start | bytes 5242880 | tf_op jit(solution)/shard_map/reduce_scatter | solution.py:188
  1419.0 398.9 %all-reduce.15.cloned.1.call-start = ((), (), s32[]{:S(2)}) async-start(), calls=%async_computation.26 | async-start | bytes 8388608 | tf_op jit(solution)/shard_map/psum | solution.py:84
  1687.3 3.2 copy-start.11
  1687.3 3.2 copy-start.7
  1687.3 3.7 copy-start.17
  1694.8 216.0 %reduce-scatter.17.cloned.1.call-start = ((), (), s32[]{:S(2)}) async-start(), calls=%async_computation.27 | async-start | bytes 4718592 | tf_op jit(solution)/shard_map/reduce_scatter | solution.py:283
  1701.1 302.1 %reduce-scatter.23.cloned.1.call-start = ((), (), s32[]{:S(2)}) async-start(), calls=%async_computation.30 | async-start | bytes 4718592 | tf_op jit(solution)/shard_map/reduce_scatter | solution.py:286
  1707.7 477.2 %reduce-scatter.25.cloned.1.call-start = ((), (), s32[]{:S(2)}) async-start(), calls=%async_computation.31 | async-start | bytes 11796480 | tf_op jit(solution)/shard_map/reduce_scatter | solution.py:211
  1716.7 649.4 %reduce-scatter.27.cloned.1.call-start = ((), (), s32[]{:S(2)}) async-start(), calls=%async_computation.32 | async-start | bytes 11796480 | tf_op jit(solution)/shard_map/reduce_scatter | solution.py:212
  1725.7 821.6 %reduce-scatter.29.cloned.1.call-start = ((), (), s32[]{:S(2)}) async-start(), calls=%async_computation.33 | async-start | bytes 11796480 | tf_op jit(solution)/shard_map/reduce_scatter | solution.py:213
  1734.6 904.1 %reduce-scatter.19.cloned.1.call-start = ((), (), s32[]{:S(2)}) async-start(), calls=%async_computation.28 | async-start | bytes 4718592 | tf_op jit(solution)/shard_map/reduce_scatter | solution.py:284
  1738.0 992.9 %reduce-scatter.21.cloned.1.call-start = ((), (), s32[]{:S(2)}) async-start(), calls=%async_computation.29 | async-start | bytes 4718592 | tf_op jit(solution)/shard_map/reduce_scatter | solution.py:285
  1742.5 75.5 %copy-start.5 = (bf16[2,256,2048]{2,1,0:T(8,128)(2,1)S(1)}, bf16[2,256,2048]{2,1,0:T(8,128)(2,1)}, u32[]{:S(2)}) copy-start(bf16[2,256,2048]{2,1,0:T(8,128)(2,1)} %all-gather.15.cloned.1.call-done) | copy-start | bytes 6291460
  1742.5 75.5 %copy-start.24 = (f32[1,2,2,128]{3,1,2,0:T(2,128)S(1)}, f32[1,2,2,128]{3,1,2,0:T(2,128)}, u32[]{:S(2)}) copy-start(f32[1,2,2,128]{3,1,2,0:T(2,128)} %copy-done.23) | copy-start | bytes 6148
  1747.9 76.6 %copy-start.25 = (f32[2048]{0:T(1024)S(1)}, f32[2048]{0:T(1024)}, u32[]{:S(2)}) copy-start(f32[2048]{0:T(1024)} %get-tuple-element.530) | copy-start | bytes 24580
  (27 other events, 49.3 us)
Sparse Core Ops, SparseCore 0:
  9.6 25.2 all-gather.14
  37.0 49.2 all-gather.18
  88.5 47.7 all-gather.22
  138.3 47.7 all-gather.16
  188.7 71.8 all-gather.20
  263.2 71.6 all-gather.24
  337.0 47.5 all-gather.26
  493.0 83.8 all-reduce.10
  579.3 86.4 all-gather.28
  668.1 84.4 all-gather.30
  754.8 20.7 all-gather.34
  777.8 86.2 all-gather.32
  884.9 83.6 all-reduce.12
  1383.1 149.0 reduce-scatter.12
  1536.1 148.0 reduce-scatter.14
  1686.6 43.4 reduce-scatter.10
  1732.4 85.4 all-reduce.14
  1822.0 88.7 reduce-scatter.16
  1915.5 87.6 reduce-scatter.22
  2007.2 177.6 reduce-scatter.24
  2189.0 177.0 reduce-scatter.26
  2370.2 176.9 reduce-scatter.28
  2551.5 87.1 reduce-scatter.18
  2643.2 87.6 reduce-scatter.20
where the time goes:
time: 2750 us; the launch traced here: 2740 us
  waiting for transfers between devices  1840 us (67%)
  local copies, waits for them, and re-layouts  453 us (16%)
  matrix products  255 us (9%)
  blocking collectives  104 us (4%)
  other arithmetic  62.8 us (2%)
    psum x3, waiting for transfers between devices, feature_total(): return lax.psum(partial_rows, 'fsdp')  217 us
    reduce_scatter x1, waiting for transfers between devices, shards(): lax.psum_scatter(grad_gate, 'seq', scatter_dimension=0, tiled=True)  182 us
    reduce_scatter x1, waiting for transfers between devices, shards(): lax.psum_scatter(grad_up, 'seq', scatter_dimension=0, tiled=True)  181 us
    reduce_scatter x1, waiting for transfers between devices, shards(): lax.psum_scatter(grad_down, 'seq', scatter_dimension=0, tiled=True)  181 us
    reduce_scatter x1, waiting for transfers between devices, shards(): lax.psum_scatter(value_terms.reshape(wide_shape), 'seq', scatter_dimensio...  149 us
    reduce_scatter x1, waiting for transfers between devices, shards(): lax.psum_scatter(key_terms.reshape(wide_shape), 'seq', scatter_dimension=...  108 us
    reduce_scatter x1, waiting for transfers between devices, shards(): lax.psum_scatter(grad_output, 'seq', scatter_dimension=0, tiled=True)  92.3 us
    reduce_scatter x1, waiting for transfers between devices, shards(): lax.psum_scatter(grad_value, 'seq', scatter_dimension=0, tiled=True)  92.2 us
  transfers between devices with their start and end apart: 24, of which 22 were waited for; matrix products, arithmetic and copies ran while one was open for 12% of the time, Pallas kernels for 0%

commit v1 on v0

--- a/solution.py
+++ b/solution.py
@@ -3,6 +3,8 @@
 import jax
 import jax.numpy as jnp
 from jax import lax
+from jax.experimental import pallas as pl
+from jax.experimental.pallas import tpu as pltpu
 from jax.sharding import PartitionSpec as P
 
 DH = 64
@@ -309,6 +311,606 @@
     )
 
 
+BLOCK = 128
+BOTH = ("seq", "fsdp")
+
+
+def move(value, target):
+    pairs = []
+    for z in range(4):
+        for y in range(2):
+            for x in range(2):
+                for c in range(2):
+                    zt, yt, xt, ct = target(z, y, x, c)
+                    pairs.append(((2 * z + y) * 4 + 2 * x + c, (2 * zt + yt) * 4 + 2 * xt + ct))
+    return lax.ppermute(value, BOTH, pairs)
+
+
+def spread_slot(k):
+    return lambda z, y, x, c: (2 * c + (k ^ (z & 1)), y, x, z >> 1)
+
+
+def spread_plane(dy, dx):
+    return lambda z, y, x, c: (z, y ^ dy, c ^ dx, x)
+
+
+def join_plane(dy, dx):
+    return lambda z, y, x, c: (z, y ^ dy, c, x ^ dx)
+
+
+def along_z(d):
+    return lambda z, y, x, c: (z ^ d, y, x, c)
+
+
+def other_core(z, y, x, c):
+    return (z, y, x, c ^ 1)
+
+
+def across(dx, dy):
+    return lambda z, y, x, c: (z, y ^ dy, x ^ dx, c)
+
+
+def across_fsdp(d):
+    return lambda z, y, x, c: (z, y, x ^ (d >> 1), c ^ (d & 1))
+
+
+def in_place(relative, me):
+    current, bit = list(relative), 1
+    while bit < len(current):
+        swap = (me & bit) != 0
+        current = [jnp.where(swap, current[i ^ bit], current[i]) for i in range(len(current))]
+        bit *= 2
+    return current
+
+
+def share_rows(rows):
+    mine = jnp.concatenate([rows] + [move(rows, along_z(d)) for d in (1, 2, 3)], axis=0)
+    return jnp.concatenate([mine, move(mine, other_core)], axis=0)
+
+
+def sum_rows(mine, other):
+    mine = mine + move(other, other_core).astype(jnp.float32)
+    count = mine.shape[0] // 4
+    total = mine[:count]
+    for d in (1, 2, 3):
+        part = mine[d * count : (d + 1) * count].astype(jnp.bfloat16)
+        total = total + move(part, along_z(d)).astype(jnp.float32)
+    return total
+
+
+def assemble_kernel(widths, *refs):
+    pieces, outs, sem = refs[:8], refs[8:-1], refs[-1]
+    z, y = lax.axis_index("seq") // 2, lax.axis_index("seq") % 2
+    x = lax.axis_index("fsdp") // 2
+    mask = 4 * x + 2 * (z % 2) + y
+    copies = []
+    for i, piece in enumerate(pieces):
+        rows = piece.shape[0]
+        first = pl.multiple_of(jnp.bitwise_xor(mask, i) * rows, rows)
+        start = 0
+        for n, (out, width) in enumerate(zip(outs, widths)):
+            copies.append(
+                pltpu.make_async_copy(
+                    piece.at[:, pl.ds(start, width)], out.at[pl.ds(first, rows), :], sem.at[i, n]
+                )
+            )
+            start += width
+    for copy in copies:
+        copy.start()
+    for copy in copies:
+        copy.wait()
+
+
+def assemble(pieces, widths):
+    rows = pieces[0].shape[0] * 8
+    return pl.pallas_call(
+        partial(assemble_kernel, widths),
+        name="assemble",
+        out_shape=[jax.ShapeDtypeStruct((rows, w), jnp.bfloat16) for w in widths],
+        in_specs=[pl.BlockSpec(memory_space=pl.ANY)] * 8,
+        out_specs=[pl.BlockSpec(memory_space=pltpu.VMEM)] * len(widths),
+        scratch_shapes=[pltpu.SemaphoreType.DMA((8, len(widths)))],
+        compiler_params=pltpu.CompilerParams(vmem_limit_bytes=24 << 20),
+    )(*pieces)
+
+
+def gather_weights(slots, widths):
+    pieces = [None] * 8
+    for k in range(2):
+        held = move(slots[k], spread_slot(k))
+        for dx in range(2):
+            for dy in range(2):
+                pieces[4 * dx + 2 * k + dy] = move(held, spread_plane(dy, dx))
+    return assemble(pieces, widths)
+
+
+def scatter_grads(grads, mask, count):
+    out = []
+    for k in range(2):
+        total = 0.0
+        for dx in range(2):
+            for dy in range(2):
+                first = ((4 * dx + 2 * k + dy) ^ mask) * count
+                part = jnp.concatenate(
+                    [lax.dynamic_slice_in_dim(g, first, count, 0) for g in grads], axis=1
+                )
+                total = total + move(part, join_plane(dy, dx)).astype(jnp.float32)
+        out.append(move(total.astype(jnp.bfloat16), spread_slot(k)).astype(jnp.float32))
+    return out
+
+
+KEYS = 256
+QUERIES = 256
+OFFSET = 1920
+
+
+def skew_table(rev_ref, table):
+    width = rev_ref.shape[1]
+    line = jnp.broadcast_to(rev_ref[...], (8, width))
+    for first in range(0, BLOCK, 8):
+        table[first : first + 8, :] = pltpu.roll(
+            line, (width - (BLOCK - 1) + first) % width, axis=1, stride=1, stride_axis=0
+        )
+
+
+def place_of(piece, part, z, y, x, c):
+    c_rel, d = part // 4, part % 4
+    b = jnp.bitwise_xor(x, piece // 2)
+    block = (
+        4 * jnp.bitwise_xor(z, d)
+        + 2 * jnp.bitwise_xor(y, piece % 2)
+        + jnp.bitwise_xor(c, c_rel)
+    )
+    return b, block
+
+
+def part_of(b, block, z, y, x, c):
+    piece = 2 * jnp.bitwise_xor(b, x) + jnp.bitwise_xor((block // 2) % 2, y)
+    part = 4 * jnp.bitwise_xor(block % 2, c) + jnp.bitwise_xor(block // 4, z)
+    return piece, part
+
+
+def lanes(first, count):
+    return pl.ds(pl.multiple_of(first, BLOCK), count)
+
+
+def attend_kernel(sc, p0, p1, p2, p3, rev_ref, ctx_ref, ctx_wide, lse_ref, qkv, keys, table):
+    z, y, x, c = sc[2], sc[3], sc[4], sc[5]
+    for piece, ref in enumerate((p0, p1, p2, p3)):
+        for part in range(8):
+            b, block = place_of(piece, part, z, y, x, c)
+            data = ref[:, :, part * BLOCK : (part + 1) * BLOCK]
+            qkv[b, :, :, lanes(block * BLOCK, BLOCK)] = data
+            keys[b, lanes(block * BLOCK, BLOCK), :] = data[1].T
+    skew_table(rev_ref, table)
+    length = qkv.shape[-1]
+    for b in range(2):
+        valid = sc[b]
+        full = valid // KEYS
+
+        @pl.loop(0, length // QUERIES)
+        def _(i):
+            first_query = i * QUERIES
+            query = qkv[b, 0, :, lanes(first_query, QUERIES)]
+
+            def tile(j, carry, masked):
+                peak, total, acc = carry
+                first_key = j * KEYS
+                score = jnp.dot(
+                    keys[b, lanes(first_key, KEYS), :], query, preferred_element_type=jnp.float32
+                )
+                score = score + jnp.concatenate(
+                    [
+                        table[:, lanes(first_query - first_key + OFFSET - t, QUERIES)]
+                        for t in range(0, KEYS, BLOCK)
+                    ],
+                    axis=0,
+                )
+                if masked:
+                    position = first_key + lax.broadcasted_iota(jnp.int32, (KEYS, QUERIES), 0)
+                    score = jnp.where(position < valid, score, masked_score)
+                now = jnp.maximum(peak, jnp.max(score, axis=0, keepdims=True))
+                scale = jnp.exp(peak - now)
+                prob = jnp.exp(score - now)
+                total = total * scale + jnp.sum(prob, axis=0, keepdims=True)
+                acc = acc * scale + jnp.dot(
+                    qkv[b, 2, :, lanes(first_key, KEYS)],
+                    prob.astype(jnp.bfloat16),
+                    preferred_element_type=jnp.float32,
+                )
+                return now, total, acc
+
+            carry = (
+                jnp.full((1, QUERIES), masked_score, jnp.float32),
+                jnp.zeros((1, QUERIES), jnp.float32),
+                jnp.zeros((DH, QUERIES), jnp.float32),
+            )
+            carry = lax.fori_loop(0, full, lambda j, s: tile(j, s, False), carry)
+            peak, total, acc = lax.cond(
+                valid > full * KEYS, lambda s: tile(full, s, True), lambda s: s, carry
+            )
+            context = acc / total
+            ctx_wide[b, :, lanes(first_query, QUERIES)] = context
+            lse_ref[b, :, lanes(first_query, QUERIES)] = peak + jnp.log(total)
+            low = context.astype(jnp.bfloat16)
+            for t in range(QUERIES // BLOCK):
+                piece, part = part_of(b, i * (QUERIES // BLOCK) + t, z, y, x, c)
+                ctx_ref[piece, :, lanes(part * BLOCK, BLOCK)] = low[:, t * BLOCK : (t + 1) * BLOCK]
+
+
+def attend(scalars, pieces, rev_line):
+    _, head_size, tokens = pieces[0].shape
+    length = tokens * 2
+    smem, vmem = pl.BlockSpec(memory_space=pltpu.SMEM), pl.BlockSpec(memory_space=pltpu.VMEM)
+    return pl.pallas_call(
+        attend_kernel,
+        name="attend",
+        out_shape=[
+            jax.ShapeDtypeStruct((4, head_size, tokens), jnp.bfloat16),
+            jax.ShapeDtypeStruct((2, head_size, length), jnp.float32),
+            jax.ShapeDtypeStruct((2, 1, length), jnp.float32),
+            jax.ShapeDtypeStruct((2, 3, head_size, length), jnp.bfloat16),
+        ],
+        in_specs=[smem] + [vmem] * 5,
+        out_specs=[vmem] * 4,
+        scratch_shapes=[
+            pltpu.VMEM((2, length, head_size), jnp.bfloat16),
+            pltpu.VMEM((BLOCK, rev_line.shape[1]), jnp.float32),
+        ],
+        compiler_params=pltpu.CompilerParams(vmem_limit_bytes=48 << 20),
+    )(scalars, *pieces, rev_line)
+
+
+def attend_back_kernel(
+    sc, p0, p1, p2, p3, rev_ref, ctx_wide, lse_ref, qkv,
+    out_ref, line_ref,
+    queries, keys, values, grads, grads_t, delta, query_sum, key_sum, value_sum, table, table_sum,
+):
+    z, y, x, c = sc[2], sc[3], sc[4], sc[5]
+    length = qkv.shape[-1]
+    for piece, ref in enumerate((p0, p1, p2, p3)):
+        for part in range(8):
+            b, block = place_of(piece, part, z, y, x, c)
+            data = ref[:, part * BLOCK : (part + 1) * BLOCK]
+            grads_t[b, :, lanes(block * BLOCK, BLOCK)] = data
+            grads[b, lanes(block * BLOCK, BLOCK), :] = data.T
+    for b in range(2):
+        for first in range(0, length, BLOCK):
+            here = slice(first, first + BLOCK)
+            queries[b, here, :] = qkv[b, 0, :, here].T
+            keys[b, here, :] = qkv[b, 1, :, here].T
+            values[b, here, :] = qkv[b, 2, :, here].T
+        delta[b] = jnp.sum(
+            ctx_wide[b] * grads_t[b].astype(jnp.float32), axis=0, keepdims=True
+        )
+    skew_table(rev_ref, table)
+    table_sum[...] = jnp.zeros_like(table_sum)
+    query_sum[...] = jnp.zeros_like(query_sum)
+    out_ref[...] = jnp.zeros_like(out_ref)
+    for b in range(2):
+        valid = sc[b]
+        full = valid // KEYS
+        count = (valid + KEYS - 1) // KEYS
+
+        def key_step(j, masked):
+            first_key = j * KEYS
+            key, value = keys[b, lanes(first_key, KEYS), :], values[b, lanes(first_key, KEYS), :]
+            key_t = qkv[b, 1, :, lanes(first_key, KEYS)]
+            key_sum[...] = jnp.zeros_like(key_sum)
+            value_sum[...] = jnp.zeros_like(value_sum)
+
+            @pl.loop(0, count)
+            def _(i):
+                first_query = i * QUERIES
+                here = lanes(first_query, QUERIES)
+                score = jnp.dot(key, qkv[b, 0, :, here], preferred_element_type=jnp.float32)
+                score = score + jnp.concatenate(
+                    [
+                        table[:, lanes(first_query - first_key + OFFSET - t, QUERIES)]
+                        for t in range(0, KEYS, BLOCK)
+                    ],
+                    axis=0,
+                )
+                if masked:
+                    position = first_key + lax.broadcasted_iota(jnp.int32, (KEYS, QUERIES), 0)
+                    score = jnp.where(position < valid, score, masked_score)
+                prob = jnp.exp(score - lse_ref[b, :, here])
+                prob_grad = jnp.dot(value, grads_t[b, :, here], preferred_element_type=jnp.float32)
+                score_grad = (prob * (prob_grad - delta[b, :, here])).astype(jnp.bfloat16)
+                value_sum[...] += jnp.dot(
+                    prob.astype(jnp.bfloat16), grads[b, here, :], preferred_element_type=jnp.float32
+                )
+                key_sum[...] += jnp.dot(
+                    score_grad, queries[b, here, :], preferred_element_type=jnp.float32
+                )
+                query_sum[b, :, here] += jnp.dot(
+                    key_t, score_grad, preferred_element_type=jnp.float32
+                )
+                for t in range(0, KEYS, BLOCK):
+                    table_sum[:, lanes(first_query - first_key + OFFSET - t, QUERIES)] += score_grad[
+                        t : t + BLOCK
+                    ].astype(jnp.float32)
+
+            for t in range(KEYS // BLOCK):
+                piece, part = part_of(b, j * (KEYS // BLOCK) + t, z, y, x, c)
+                rows = slice(t * BLOCK, (t + 1) * BLOCK)
+                at = lanes(part * BLOCK, BLOCK)
+                out_ref[piece, 1, :, at] = key_sum[rows, :].T.astype(jnp.bfloat16)
+                out_ref[piece, 2, :, at] = value_sum[rows, :].T.astype(jnp.bfloat16)
+
+        pl.loop(0, full)(lambda j: key_step(j, False))
+        pl.when(valid > full * KEYS)(lambda: key_step(full, True))
+        for block in range(length // BLOCK):
+            piece, part = part_of(b, block, z, y, x, c)
+            out_ref[piece, 0, :, lanes(part * BLOCK, BLOCK)] = query_sum[
+                b, :, block * BLOCK : (block + 1) * BLOCK
+            ].astype(jnp.bfloat16)
+    width = table_sum.shape[1]
+    line = jnp.zeros((8, width), jnp.float32)
+    for first in range(0, BLOCK, 8):
+        line = line + pltpu.roll(table_sum[first : first + 8, :], BLOCK - 8 - first, axis=1)
+    ahead = 7 - lax.broadcasted_iota(jnp.int32, (8, width), 0)
+    for bit in (1, 2, 4):
+        line = jnp.where((ahead & bit) != 0, pltpu.roll(line, bit, axis=1), line)
+    line_ref[...] = jnp.sum(line, axis=0, keepdims=True)
+
+
+def attend_back(scalars, pieces, rev_line, ctx_wide, lse, qkv):
+    head_size, tokens = pieces[0].shape
+    length = tokens * 2
+    smem, vmem = pl.BlockSpec(memory_space=pltpu.SMEM), pl.BlockSpec(memory_space=pltpu.VMEM)
+    low = pltpu.VMEM((2, length, head_size), jnp.bfloat16)
+    return pl.pallas_call(
+        attend_back_kernel,
+        name="attend_back",
+        out_shape=[
+            jax.ShapeDtypeStruct((4, 3, head_size, tokens), jnp.bfloat16),
+            jax.ShapeDtypeStruct(rev_line.shape, jnp.float32),
+        ],
+        in_specs=[smem] + [vmem] * 8,
+        out_specs=[vmem] * 2,
+        scratch_shapes=[
+            low, low, low, low,
+            pltpu.VMEM((2, head_size, length), jnp.bfloat16),
+            pltpu.VMEM((2, 1, length), jnp.float32),
+            pltpu.VMEM((2, head_size, length), jnp.float32),
+            pltpu.VMEM((KEYS, head_size), jnp.float32),
+            pltpu.VMEM((KEYS, head_size), jnp.float32),
+            pltpu.VMEM((BLOCK, rev_line.shape[1]), jnp.float32),
+            pltpu.VMEM((BLOCK, rev_line.shape[1]), jnp.float32),
+        ],
+        compiler_params=pltpu.CompilerParams(vmem_limit_bytes=48 << 20),
+    )(scalars, *pieces, rev_line, ctx_wide, lse, qkv)
+
+
+def fast_shards(
+    tokens_in,
+    cotangent,
+    gain_attn,
+    query_weight,
+    key_weight,
+    value_weight,
+    output_weight,
+    bias_table,
+    gain_ffn,
+    gate_weight,
+    up_weight,
+    down_weight,
+    lengths,
+    buckets,
+):
+    seq_index, fsdp_index = lax.axis_index("seq"), lax.axis_index("fsdp")
+    z, y, x, c = seq_index // 2, seq_index % 2, fsdp_index // 2, fsdp_index % 2
+    z_low, z_high = z % 2, z // 2
+    batch_count, slot_count, part_width = tokens_in.shape
+    width = part_width * 4
+    row_count = query_weight.shape[0]
+    heads = query_weight.shape[1] // DH
+    group_heads = heads // 2
+    group_width = group_heads * DH
+    hidden_width = gate_weight.shape[1] // 2
+    scalars = jnp.concatenate(
+        [lengths, jnp.stack([z, y, x, c]).astype(jnp.int32), jnp.zeros((2,), jnp.int32)]
+    )
+    mask = 4 * x + 2 * z_low + y
+
+    def halves(weights):
+        slots = []
+        for k in range(2):
+            half = k ^ z_low
+            slots.append(
+                jnp.concatenate(
+                    [
+                        lax.dynamic_slice_in_dim(w, half * (w.shape[1] // 2), w.shape[1] // 2, 1)
+                        for w in weights
+                    ],
+                    axis=1,
+                )
+            )
+        return slots
+
+    small = jnp.concatenate([gain_attn, gain_ffn, bias_table.reshape(-1)])[None]
+    for d in range(3):
+        small = jnp.concatenate(
+            [small, move(small, (across(0, 1), along_z(1), along_z(2))[d])], axis=0
+        )
+    small = jnp.stack(in_place([small[i] for i in range(8)], seq_index))
+    gain_one = small[:, :row_count].reshape(-1)
+    gain_two = small[:, row_count : 2 * row_count].reshape(-1)
+    tables = small[:, 2 * row_count :][None]
+    for d in range(2):
+        tables = jnp.concatenate([tables, move(tables, across_fsdp(1 << d))], axis=0)
+    tables = jnp.stack(in_place([tables[i] for i in range(4)], fsdp_index))
+    tables = tables.reshape(4, 8, -1, heads).transpose(1, 2, 0, 3).reshape(-1, 4 * heads)
+    own_head = (2 * c + z_high) * heads + z_low * group_heads + 2 * x + y
+    table_column = lax.dynamic_slice_in_dim(tables, own_head, 1, 1)[:, 0].astype(jnp.float32)
+    line_length = buckets.shape[0]
+    rev_buckets = jnp.concatenate([buckets[::-1], jnp.full((1,), -1, jnp.int32)])
+    bucket_hot = rev_buckets[:, None] == jnp.arange(table_column.shape[0], dtype=jnp.int32)[None, :]
+    rev_line = jnp.sum(jnp.where(bucket_hot, table_column[None, :], 0.0), axis=1)[None, :]
+
+    def own_rows(block):
+        parts = block.reshape(4, slot_count // 2, part_width)
+        got = [lax.dynamic_index_in_dim(parts, fsdp_index, 0, False)]
+        for d in (1, 2, 3):
+            piece = lax.dynamic_index_in_dim(parts, fsdp_index ^ d, 0, False)
+            got.append(move(piece, across_fsdp(d)))
+        return jnp.concatenate(in_place(got, fsdp_index), axis=1)
+
+    def home_rows(rows):
+        got = []
+        for d in range(4):
+            piece = lax.dynamic_slice_in_dim(rows, (fsdp_index ^ d) * part_width, part_width, 1)
+            got.append(piece if d == 0 else move(piece, across_fsdp(d)))
+        return jnp.stack(in_place(got, fsdp_index)).reshape(batch_count, slot_count, part_width)
+
+    first_slot = seq_index * slot_count + c * (slot_count // 2)
+    own_slots = first_slot + jnp.arange(slot_count // 2, dtype=jnp.int32)
+    own_valid = own_slots < lax.dynamic_index_in_dim(lengths, x, 0, False)
+    token_rows = own_rows(tokens_in).astype(jnp.float32)
+    (qkv_weight,) = gather_weights(
+        halves([query_weight, key_weight, value_weight]), [3 * group_width]
+    )
+    unit_one, scale_one, normed_own = normalize(token_rows, gain_one)
+    normed_one = share_rows(normed_own)
+    qkv = lax.dot_general(
+        qkv_weight, normed_one, (((0,), (1,)), ((), ())), preferred_element_type=jnp.float32
+    ).astype(jnp.bfloat16)
+    tokens = qkv.shape[1]
+    qkv = qkv.reshape(3, group_heads, DH, tokens)
+    own = 2 * x + y
+
+    def to_heads_owner(parts, axis):
+        got = []
+        for d in range(4):
+            piece = lax.dynamic_index_in_dim(parts, own ^ d, axis, False)
+            got.append(piece if d == 0 else move(piece, across(d // 2, d % 2)))
+        return got
+
+    pieces = to_heads_owner(qkv, 1)
+    context_pieces, context_wide, lse, qkv_all = attend(scalars, pieces, rev_line)
+
+    output_full, gate_up, down_full = gather_weights(
+        halves([output_weight, gate_weight, up_weight, down_weight]),
+        [group_width, 2 * hidden_width, hidden_width],
+    )
+    grad_own = jnp.where(own_valid[:, None], own_rows(cotangent), jnp.zeros((), jnp.bfloat16))
+    grad_rows = share_rows(grad_own)
+
+    def from_heads_owner(parts):
+        got = [parts[0]] + [move(parts[d], across(d // 2, d % 2)) for d in (1, 2, 3)]
+        return in_place(got, own)
+
+    context = jnp.concatenate(from_heads_owner(context_pieces), axis=0)
+    half_rows = tokens // 2
+
+    def product_rows(left, right, dims):
+        axis = 1 - dims[0]
+        first, second = (
+            lax.slice_in_dim(left, 0, half_rows, axis=axis),
+            lax.slice_in_dim(left, half_rows, tokens, axis=axis),
+        )
+        run = lambda part: lax.dot_general(
+            part, right, (((dims[0],), (dims[1],)), ((), ())), preferred_element_type=jnp.float32
+        )
+        return run(first), run(second).astype(jnp.bfloat16)
+
+    residual = token_rows + sum_rows(*product_rows(context, output_full, (0, 1)))
+    unit_two, scale_two, normed_two_own = normalize(residual, gain_two)
+    normed_two = share_rows(normed_two_own)
+    gate_up_pre = plain_product(normed_two, gate_up)
+    gate_pre, up_pre = gate_up_pre[:, :hidden_width], gate_up_pre[:, hidden_width:]
+    activated, gelu_back = jax.vjp(jax.nn.gelu, gate_pre)
+    hidden = (activated * up_pre).astype(jnp.bfloat16)
+    grad_hidden = plain_product(grad_rows, down_full)
+    grad_pre = jnp.concatenate(
+        [
+            gelu_back(grad_hidden * up_pre)[0].astype(jnp.bfloat16),
+            (grad_hidden * activated).astype(jnp.bfloat16),
+        ],
+        axis=1,
+    )
+    normed_two_grad = sum_rows(*product_rows(grad_pre, gate_up, (1, 1)))
+    residual_grad = grad_own.astype(jnp.float32) + norm_back(
+        normed_two_grad, unit_two, scale_two, gain_two
+    )
+    residual_low = share_rows(residual_grad.astype(jnp.bfloat16))
+    context_grad = lax.dot_general(
+        output_full, residual_low, (((0,), (1,)), ((), ())), preferred_element_type=jnp.float32
+    ).astype(jnp.bfloat16)
+    grad_pieces = to_heads_owner(context_grad.reshape(group_heads, DH, tokens), 0)
+    qkv_grad_pieces, line_grad = attend_back(
+        scalars, grad_pieces, rev_line, context_wide, lse, qkv_all
+    )
+
+    grad_gate_up = left_transposed(normed_two, grad_pre).astype(jnp.bfloat16)
+    grad_down = left_transposed(grad_rows, hidden).astype(jnp.bfloat16)
+    grad_output = lax.dot_general(
+        residual_low, context, (((0,), (1,)), ((), ())), preferred_element_type=jnp.float32
+    ).astype(jnp.bfloat16)
+    ffn_share = sum_rows(*product_rows(hidden, down_full, (1, 1)))
+    layer_out = home_rows((residual + ffn_share).astype(jnp.bfloat16))
+
+    def own_columns(slots, first, size):
+        cut = [s[:, first : first + size] for s in slots]
+        return jnp.concatenate(
+            [jnp.where(z_low == 0, cut[0], cut[1]), jnp.where(z_low == 0, cut[1], cut[0])], axis=1
+        )
+
+    ffn_sums = scatter_grads([grad_output, grad_gate_up, grad_down], mask, row_count)
+    output_sum = own_columns(ffn_sums, 0, group_width)
+    gate_sum = own_columns(ffn_sums, group_width, hidden_width)
+    up_sum = own_columns(ffn_sums, group_width + hidden_width, hidden_width)
+    down_sum = own_columns(ffn_sums, group_width + 2 * hidden_width, hidden_width)
+
+    qkv_grad = jnp.stack(from_heads_owner(qkv_grad_pieces), axis=1).reshape(3 * group_width, tokens)
+    grad_qkv = lax.dot_general(
+        normed_one, qkv_grad, (((0,), (1,)), ((), ())), preferred_element_type=jnp.float32
+    ).astype(jnp.bfloat16)
+    normed_one_grad = sum_rows(*product_rows(qkv_grad, qkv_weight, (0, 1)))
+    qkv_sums = scatter_grads([grad_qkv], mask, row_count)
+    query_sum = own_columns(qkv_sums, 0, group_width)
+    key_sum = own_columns(qkv_sums, group_width, group_width)
+    value_sum = own_columns(qkv_sums, 2 * group_width, group_width)
+    token_grad = residual_grad + norm_back(normed_one_grad, unit_one, scale_one, gain_one)
+    token_share = home_rows(token_grad)
+
+    table_grad = jnp.sum(jnp.where(bucket_hot, line_grad[0][:, None], 0.0), axis=0)
+    head_hot = (jnp.arange(4 * heads) == own_head).astype(jnp.float32)
+    packed = jnp.concatenate(
+        [
+            jnp.sum(normed_one_grad * unit_one, axis=0).reshape(8, row_count),
+            jnp.sum(normed_two_grad * unit_two, axis=0).reshape(8, row_count),
+            (table_grad[:, None] * head_hot[None, :]).reshape(8, -1),
+        ],
+        axis=1,
+    )
+    for index, size, way in ((z_high, 4, along_z(2)), (z_low, 2, along_z(1)), (y, 1, across(0, 1))):
+        kept = lax.dynamic_slice_in_dim(packed, index * size, size, 0)
+        sent = lax.dynamic_slice_in_dim(packed, (1 - index) * size, size, 0)
+        packed = kept + move(sent, way)
+    for d in range(2):
+        packed = packed + move(packed, across_fsdp(1 << d))
+    packed = packed[0]
+    table_sum = lax.dynamic_slice_in_dim(
+        packed[2 * row_count :].reshape(-1, 4 * heads), fsdp_index * heads, heads, 1
+    )
+    return (
+        layer_out,
+        token_share,
+        packed[:row_count],
+        query_sum,
+        key_sum,
+        value_sum,
+        output_sum,
+        table_sum,
+        packed[row_count : 2 * row_count],
+        gate_sum,
+        up_sum,
+        down_sum,
+    )
+
+
 def solution(mesh):
     placed = (
         P(None, "seq", "fsdp"),
@@ -327,7 +929,7 @@
         P(),
     )
     return jax.shard_map(
-        shards,
+        fast_shards if (mesh.shape["seq"], mesh.shape["fsdp"]) == (8, 4) else shards,
         mesh=mesh,
         in_specs=placed,
         out_specs=(

time: 2750 us -> 981 us (0.36)
  waiting for transfers between devices: 1840 us -> 440 us
  local copies, waits for them, and re-layouts: 453 us -> 43 us
  starting transfers between devices: 1.22 us -> 279 us
  matrix products: 255 us -> 58.6 us
  blocking collectives: 104 us -> 0 us
  Pallas kernels: 0 us -> 102 us
    reduce_scatter x10 -> x0, waiting for transfers between devices: 1110 us -> none  [the longest x1 182 us: shards(): lax.psum_scatter(grad_gate, 'seq', scatter_dimension=0, tiled=True)]
    all_gather x11 -> x0, waiting for transfers between devices: 507 us -> none  [the longest x1 88.6 us: shards(): lax.all_gather(down_weight, 'seq', axis=0, tiled=True)]
    ppermute x0 -> x106, waiting for transfers between devices: none -> 440 us  [move(): return lax.ppermute(value, BOTH, pairs)]
    ppermute x0 -> x106, starting transfers between devices: none -> 279 us  [move(): return lax.ppermute(value, BOTH, pairs)]
    psum x3 -> x0, waiting for transfers between devices: 217 us -> none  [feature_total(): return lax.psum(partial_rows, 'fsdp')]
    reshape x42 -> x5, local copies, waits for them, and re-layouts: 185 us -> 0.94 us  [the longest x1 0.76 us: fast_shards(): small = jnp.concatenate([gain_attn, gain_ffn, bias_table.reshape(-1)])[None]]
    dot_general x65 -> x12, matrix products: 179 us -> 36.5 us  [the longest x8 26.3 us: product_rows(): lax.dot_general(part, right, (((dims[0],), (dims[1],)), ((), ())), prefer...]
    pallas_call x0 -> x4, Pallas kernels: none -> 102 us  [the longest x1 49.8 us: attend(): pl.pallas_call(attend_kernel, name='attend', out_shape=[jax.ShapeDtypeStr...]
  transfers between devices with their start and end apart: 24 -> 106, of which waited for: 22 -> 45; matrix products, arithmetic and copies ran while one was open for 12% -> 9% of each run, Pallas kernels for 0% -> 6%
where the time goes in v1:
time: 981 us; the launch traced here: 972 us
  waiting for transfers between devices  440 us (45%)
  starting transfers between devices  279 us (28%)
  Pallas kernels  102 us (10%)
  matrix products  58.6 us (6%)
  other arithmetic  45.9 us (5%)
  local copies, waits for them, and re-layouts  43 us (4%)
    ppermute x106, waiting for transfers between devices, move(): return lax.ppermute(value, BOTH, pairs)  440 us
    ppermute x106, starting transfers between devices, move(): return lax.ppermute(value, BOTH, pairs)  279 us
    pallas_call x1, Pallas kernels, attend(): pl.pallas_call(attend_kernel, name='attend', out_shape=[jax.ShapeDtypeStr...  49.8 us
    pallas_call x1, Pallas kernels, attend_back(): pl.pallas_call(attend_back_kernel, name='attend_back', out_shape=[jax.Sha...  48.2 us
    dot_general x8, matrix products, product_rows(): lax.dot_general(part, right, (((dims[0],), (dims[1],)), ((), ())), prefer...  26.3 us
    unnamed x202, local copies, waits for them, and re-layouts  23.1 us
  transfers between devices with their start and end apart: 106, of which 45 were waited for; matrix products, arithmetic and copies ran while one was open for 9% of the time, Pallas kernels for 6%

profile of v1, /device:TPU:0, one launch (start us, length us, event | category | flops | bytes accessed | tf_op | source)
XLA Modules:
  0.0 971.7 jit_solution(9051515245788749275)
XLA Ops:
  36.8 12.8 %collective-permute-done.16 = bf16[128,2048]{1,0:T(8,128)(2,1)S(1)} collective-permute-done((bf16[128,2048]{1,0:T(8,128)(2,1)S(1)}, bf16[128,2048]{1,0:T(8,128)(2,1)S(1)}, u32[]{:S(2)}, u32[]{:S(2)}) %collective-permute-start.16) | collective-permute-done | bytes 524320 | tf_op jit(solution)/shard_map/ppermute | solution.py:326
  49.7 19.8 %collective-permute-done.17 = bf16[128,2048]{1,0:T(8,128)(2,1)S(1)} collective-permute-done((bf16[128,2048]{1,0:T(8,128)(2,1)S(1)}, bf16[128,2048]{1,0:T(8,128)(2,1)S(1)}, u32[]{:S(2)}, u32[]{:S(2)}) %collective-permute-start.17) | collective-permute-done | bytes 524320 | tf_op jit(solution)/shard_map/ppermute | solution.py:326
  71.7 4.5 collective-permute-start.3
  78.4 15.2 %collective-permute-start.12 = (bf16[256,768]{1,0:T(8,128)(2,1)}, bf16[256,768]{1,0:T(8,128)(2,1)S(1)}, u32[]{:S(2)}, u32[]{:S(2)}) collective-permute-start(bf16[256,768]{1,0:T(8,128)(2,1)} %collective-permute-done.6), channel_id=1, source_target_pairs={{0,6},{1,4},{2,7},{3,5},{4,2},{5,0},{6,3},{7,1},{8,14},{9,12},{10,... | collective-permute-start | bytes 1179656 | tf_op jit(solution)/shard_map/ppermute | solution.py:326
  99.2 7.0 collective-permute-start.10
  112.0 9.4 collective-permute-done.10.refs_5_
  136.7 5.5 collective-permute-start.36
  150.3 8.4 collective-permute-start.22
  159.7 30.0 %collective-permute-start.37 = (bf16[256,2176]{1,0:T(8,128)(2,1)}, bf16[256,2176]{1,0:T(8,128)(2,1)}, u32[]{:S(2)}, u32[]{:S(2)}) collective-permute-start(bf16[256,2176]{1,0:T(8,128)(2,1)} %collective-permute-done.31), channel_id=1, source_target_pairs={{0,6},{1,4},{2,7},{3,5},{4,2},{5,0},{6,3},{7,1},{8,14},{9,12},{10,... | collective-permute-start | bytes 3342344 | tf_op jit(solution)/shard_map/ppermute | solution.py:326
  190.7 9.8 %collective-permute-start.29 = (bf16[256,2176]{1,0:T(8,128)(2,1)}, bf16[256,2176]{1,0:T(8,128)(2,1)}, u32[]{:S(2)}, u32[]{:S(2)}) collective-permute-start(bf16[256,2176]{1,0:T(8,128)(2,1)} %collective-permute-done.28), channel_id=1, source_target_pairs={{0,0},{1,2},{2,1},{3,3},{4,4},{5,6},{6,5},{7,7},{8,8},{9,10},{10,9... | collective-permute-start | bytes 3342344 | tf_op jit(solution)/shard_map/ppermute | solution.py:326
  206.7 49.8 %attend.1 = (bf16[4,64,1024]{2,1,0:T(8,128)(2,1)S(1)}, f32[2,64,2048]{2,1,0:T(8,128)S(1)}, f32[2,1,2048]{2,1,0:T(1,128)S(1)}, bf16[2,3,64,2048]{3,2,1,0:T(8,128)(2,1)S(1)}) custom-call(s32[8]{0:T(128)S(1)} %copy-done.17, bf16[3,64,1024]{2,1,0:T(8,128)(2,1)S(1)} %get-tuple-element.123.p0, bf16[3,64,1024]{2,1,0:T(8,128)(2,1)S(1)} %collective-permute-done.20.p1, ...), custom_call_target="tpu_custom_call" | custom-call | tf_op jit(solution)/shard_map/attend/pallas_call | solution.py:545
  261.7 7.0 collective-permute-done.35.refs_5_
  285.1 5.0 collective-permute-start.57
  297.2 12.9 %collective-permute-done.56 = bf16[128,2048]{1,0:T(8,128)(2,1)S(1)} collective-permute-done((bf16[128,2048]{1,0:T(8,128)(2,1)S(1)}, bf16[128,2048]{1,0:T(8,128)(2,1)S(1)}, u32[]{:S(2)}, u32[]{:S(2)}) %collective-permute-start.56) | collective-permute-done | bytes 524320 | tf_op jit(solution)/shard_map/ppermute | solution.py:326
  310.4 16.4 %collective-permute-done.58 = bf16[128,2048]{1,0:T(8,128)(2,1)S(1)} collective-permute-done((bf16[128,2048]{1,0:T(8,128)(2,1)S(1)}, bf16[128,2048]{1,0:T(8,128)(2,1)S(1)}, u32[]{:S(2)}, u32[]{:S(2)}) %collective-permute-start.58) | collective-permute-done | bytes 524320 | tf_op jit(solution)/shard_map/ppermute | solution.py:326
  327.0 5.2 collective-permute-done.39
  332.2 38.1 %collective-permute-done.40 = bf16[128,2048]{1,0:T(8,128)(2,1)S(1)} collective-permute-done((bf16[128,2048]{1,0:T(8,128)(2,1)S(1)}, bf16[128,2048]{1,0:T(8,128)(2,1)S(1)}, u32[]{:S(2)}, u32[]{:S(2)}) %collective-permute-start.40) | collective-permute-done | bytes 524320 | tf_op jit(solution)/shard_map/ppermute | solution.py:326
  371.1 12.1 %collective-permute-start.42 = (bf16[128,2048]{1,0:T(8,128)(2,1)S(1)}, bf16[128,2048]{1,0:T(8,128)(2,1)S(1)}, u32[]{:S(2)}, u32[]{:S(2)}) collective-permute-start(bf16[128,2048]{1,0:T(8,128)(2,1)S(1)} %get-tuple-element.41), channel_id=1, source_target_pairs={{0,8},{1,9},{2,10},{3,11},{4,12},{5,13},{6,14},{7,15},{8,0},{9,1},... | collective-permute-start | bytes 1572872 | tf_op jit(solution)/shard_map/ppermute | solution.py:326
  386.5 18.9 %collective-permute-done.42 = bf16[128,2048]{1,0:T(8,128)(2,1)S(1)} collective-permute-done((bf16[128,2048]{1,0:T(8,128)(2,1)S(1)}, bf16[128,2048]{1,0:T(8,128)(2,1)S(1)}, u32[]{:S(2)}, u32[]{:S(2)}) %collective-permute-start.42) | collective-permute-done | bytes 524320 | tf_op jit(solution)/shard_map/ppermute | solution.py:326
  405.5 15.9 %collective-permute-done.43 = bf16[128,2048]{1,0:T(8,128)(2,1)S(1)} collective-permute-done((bf16[128,2048]{1,0:T(8,128)(2,1)S(1)}, bf16[128,2048]{1,0:T(8,128)(2,1)S(1)}, u32[]{:S(2)}, u32[]{:S(2)}) %collective-permute-start.43) | collective-permute-done | bytes 524320 | tf_op jit(solution)/shard_map/ppermute | solution.py:326
  425.9 5.6 fusion.58
  431.6 6.3 multiply_convert_fusion
  445.3 4.4 fusion.55
  450.9 10.1 %collective-permute-start.61 = (bf16[128,2048]{1,0:T(8,128)(2,1)}, bf16[128,2048]{1,0:T(8,128)(2,1)}, u32[]{:S(2)}, u32[]{:S(2)}) collective-permute-start(bf16[128,2048]{1,0:T(8,128)(2,1)} %get-tuple-element.98), channel_id=1, source_target_pairs={{0,8},{1,9},{2,10},{3,11},{4,12},{5,13},{6,14},{7,15},{8,0},{9,1},... | collective-permute-start | bytes 1572872 | tf_op jit(solution)/shard_map/ppermute | solution.py:326
  468.3 16.2 %collective-permute-done.61 = bf16[128,2048]{1,0:T(8,128)(2,1)} collective-permute-done((bf16[128,2048]{1,0:T(8,128)(2,1)}, bf16[128,2048]{1,0:T(8,128)(2,1)}, u32[]{:S(2)}, u32[]{:S(2)}) %collective-permute-start.61) | collective-permute-done | bytes 524320 | tf_op jit(solution)/shard_map/ppermute | solution.py:326
  484.5 14.9 %collective-permute-done.62 = bf16[128,2048]{1,0:T(8,128)(2,1)} collective-permute-done((bf16[128,2048]{1,0:T(8,128)(2,1)}, bf16[128,2048]{1,0:T(8,128)(2,1)}, u32[]{:S(2)}, u32[]{:S(2)}) %collective-permute-start.62) | collective-permute-done | bytes 524320 | tf_op jit(solution)/shard_map/ppermute | solution.py:326
  502.8 10.7 %collective-permute-start.64 = (bf16[128,2048]{1,0:T(8,128)(2,1)S(1)}, bf16[128,2048]{1,0:T(8,128)(2,1)S(1)}, u32[]{:S(2)}, u32[]{:S(2)}) collective-permute-start(bf16[128,2048]{1,0:T(8,128)(2,1)S(1)} %get-tuple-element.36), channel_id=1, source_target_pairs={{0,8},{1,9},{2,10},{3,11},{4,12},{5,13},{6,14},{7,15},{8,0},{9,1},... | collective-permute-start | bytes 1572872 | tf_op jit(solution)/shard_map/ppermute | solution.py:326
  516.8 6.1 convolution_convert_fusion
  522.9 12.2 %collective-permute-done.64 = bf16[128,2048]{1,0:T(8,128)(2,1)S(1)} collective-permute-done((bf16[128,2048]{1,0:T(8,128)(2,1)S(1)}, bf16[128,2048]{1,0:T(8,128)(2,1)S(1)}, u32[]{:S(2)}, u32[]{:S(2)}) %collective-permute-start.64) | collective-permute-done | bytes 524320 | tf_op jit(solution)/shard_map/ppermute | solution.py:326
  535.1 16.6 %collective-permute-done.65 = bf16[128,2048]{1,0:T(8,128)(2,1)S(1)} collective-permute-done((bf16[128,2048]{1,0:T(8,128)(2,1)S(1)}, bf16[128,2048]{1,0:T(8,128)(2,1)S(1)}, u32[]{:S(2)}, u32[]{:S(2)}) %collective-permute-start.65) | collective-permute-done | bytes 524320 | tf_op jit(solution)/shard_map/ppermute | solution.py:326
  578.5 48.2 %attend_back.1 = (bf16[4,3,64,1024]{3,2,1,0:T(8,128)(2,1)S(1)}, f32[1,4096]{1,0:T(1,128)S(1)}) custom-call(s32[8]{0:T(128)S(1)} %copy-done.18, bf16[64,1024]{1,0:T(8,128)(2,1)S(1)} %get-tuple-element.162.p0, bf16[64,1024]{1,0:T(8,128)(2,1)S(1)} %collective-permute-done.68.p1, bf16[64,1024]{1,0:T(8,128)(2,1)S(1)} %collective-permute-done.69.p2, ...), custom_call_target="tpu_custom_call" | custom-call | tf_op jit(solution)/shard_map/attend_back/pallas_call | solution.py:663
  630.6 9.3 collective-permute-done.71
  639.9 7.0 collective-permute-done.72
  663.5 8.4 collective-permute-done.88
  680.6 5.0 collective-permute-start.99
  685.7 39.0 %collective-permute-done.93 = bf16[256,768]{1,0:T(8,128)(2,1)S(1)} collective-permute-done((bf16[256,768]{1,0:T(8,128)(2,1)S(1)}, bf16[256,768]{1,0:T(8,128)(2,1)S(1)}, u32[]{:S(2)}, u32[]{:S(2)}) %collective-permute-start.93) | collective-permute-done | bytes 393248 | tf_op jit(solution)/shard_map/ppermute | solution.py:326
  728.8 15.2 %collective-permute-done.94 = bf16[256,768]{1,0:T(8,128)(2,1)S(1)} collective-permute-done((bf16[256,768]{1,0:T(8,128)(2,1)S(1)}, bf16[256,768]{1,0:T(8,128)(2,1)S(1)}, u32[]{:S(2)}, u32[]{:S(2)}) %collective-permute-start.94) | collective-permute-done | bytes 393248 | tf_op jit(solution)/shard_map/ppermute | solution.py:326
  753.6 4.5 collective-permute-start.90
  760.4 9.6 collective-permute-start.95
  770.0 16.6 %collective-permute-done.103 = bf16[256,2176]{1,0:T(8,128)(2,1)S(1)} collective-permute-done((bf16[256,2176]{1,0:T(8,128)(2,1)S(1)}, bf16[256,2176]{1,0:T(8,128)(2,1)S(1)}, u32[]{:S(2)}, u32[]{:S(2)}) %collective-permute-start.103) | collective-permute-done | bytes 1114144 | tf_op jit(solution)/shard_map/ppermute | solution.py:326
  786.6 10.0 %collective-permute-start.100 = (bf16[256,2176]{1,0:T(8,128)(2,1)}, bf16[256,2176]{1,0:T(8,128)(2,1)}, u32[]{:S(2)}, u32[]{:S(2)}) collective-permute-start(bf16[256,2176]{1,0:T(8,128)(2,1)} %add_convert_fusion.1), channel_id=1, source_target_pairs={{0,0},{1,16},{2,2},{3,18},{4,4},{5,20},{6,6},{7,22},{8,8},{9,24},{... | collective-permute-start | bytes 3342344 | tf_op jit(solution)/shard_map/ppermute | solution.py:326
  800.2 9.6 collective-permute-start.105
  819.6 39.0 %collective-permute-done.105 = bf16[256,2176]{1,0:T(8,128)(2,1)} collective-permute-done((bf16[256,2176]{1,0:T(8,128)(2,1)}, bf16[256,2176]{1,0:T(8,128)(2,1)}, u32[]{:S(2)}, u32[]{:S(2)}) %collective-permute-start.105) | collective-permute-done | bytes 1114144 | tf_op jit(solution)/shard_map/ppermute | solution.py:326
  866.3 5.6 collective-permute-start.76
  875.2 9.2 collective-permute-done.75
  887.0 29.1 %collective-permute-done.76 = bf16[128,2048]{1,0:T(8,128)(2,1)S(1)} collective-permute-done((bf16[128,2048]{1,0:T(8,128)(2,1)S(1)}, bf16[128,2048]{1,0:T(8,128)(2,1)S(1)}, u32[]{:S(2)}, u32[]{:S(2)}) %collective-permute-start.76) | collective-permute-done | bytes 524320 | tf_op jit(solution)/shard_map/ppermute | solution.py:326
  917.7 16.9 %collective-permute-start.81 = (f32[4,640]{1,0:T(4,128)S(1)}, f32[4,640]{1,0:T(4,128)S(1)}, u32[]{:S(2)}, u32[]{:S(2)}) collective-permute-start(f32[4,640]{1,0:T(4,128)S(1)} %constant_dynamic-slice_fusion.37), channel_id=1, source_target_pairs={{0,16},{1,17},{2,18},{3,19},{4,20},{5,21},{6,22},{7,23},{8,24},{9,... | collective-permute-start | bytes 30728 | tf_op jit(solution)/shard_map/ppermute | solution.py:326
  952.4 10.2 %collective-permute-done.85 = f32[1,640]{1,0:T(1,128)S(1)} collective-permute-done((f32[1,640]{1,0:T(1,128)S(1)}, f32[1,640]{1,0:T(1,128)S(1)}, u32[]{:S(2)}, u32[]{:S(2)}) %collective-permute-start.85) | collective-permute-done | bytes 2592 | tf_op jit(solution)/shard_map/ppermute | solution.py:326
  (519 shorter events, 269.7 us)
Async XLA Ops:
  30.8 38.6 %collective-permute-start.17 = (bf16[128,2048]{1,0:T(8,128)(2,1)S(1)}, bf16[128,2048]{1,0:T(8,128)(2,1)S(1)}, u32[]{:S(2)}, u32[]{:S(2)}) collective-permute-start(bf16[128,2048]{1,0:T(8,128)(2,1)S(1)} %get-tuple-element.45), channel_id=1, source_target_pairs={{0,16},{1,17},{2,18},{3,19},{4,20},{5,21},{6,22},{7,23},{8,24},{9,... | collective-permute-start | bytes 1572872 | tf_op jit(solution)/shard_map/ppermute | solution.py:326
  33.4 36.1 %collective-permute-start.18 = (bf16[128,2048]{1,0:T(8,128)(2,1)S(1)}, bf16[128,2048]{1,0:T(8,128)(2,1)S(1)}, u32[]{:S(2)}, u32[]{:S(2)}) collective-permute-start(bf16[128,2048]{1,0:T(8,128)(2,1)S(1)} %get-tuple-element.45), channel_id=1, source_target_pairs={{0,24},{1,25},{2,26},{3,27},{4,28},{5,29},{6,30},{7,31},{8,16},{9,... | collective-permute-start | bytes 1572872 | tf_op jit(solution)/shard_map/ppermute | solution.py:326
  36.1 41.5 %collective-permute-start.6 = (bf16[256,768]{1,0:T(8,128)(2,1)}, bf16[256,768]{1,0:T(8,128)(2,1)}, u32[]{:S(2)}, u32[]{:S(2)}) collective-permute-start(bf16[256,768]{1,0:T(8,128)(2,1)} %pad_maximum_fusion.29), channel_id=1, source_target_pairs={{0,8},{1,24},{2,10},{3,26},{4,12},{5,28},{6,14},{7,30},{8,0},{9,16... | collective-permute-start | bytes 1179656 | tf_op jit(solution)/shard_map/ppermute | solution.py:326
  70.9 65.8 %collective-permute-start.19 = (bf16[512,2048]{1,0:T(8,128)(2,1)}, bf16[512,2048]{1,0:T(8,128)(2,1)}, u32[]{:S(2)}, u32[]{:S(2)}) collective-permute-start(bf16[512,2048]{1,0:T(8,128)(2,1)} %pad_maximum_fusion.2), channel_id=1, source_target_pairs={{0,1},{1,0},{2,3},{3,2},{4,5},{5,4},{6,7},{7,6},{8,9},{9,8},{10,11... | collective-permute-start | bytes 6291464 | tf_op jit(solution)/shard_map/ppermute | solution.py:326
  94.7 37.1 %collective-permute-start.31 = (bf16[256,2176]{1,0:T(8,128)(2,1)}, bf16[256,2176]{1,0:T(8,128)(2,1)}, u32[]{:S(2)}, u32[]{:S(2)}) collective-permute-start(bf16[256,2176]{1,0:T(8,128)(2,1)} %pad_maximum_fusion.11), channel_id=1, source_target_pairs={{0,8},{1,24},{2,10},{3,26},{4,12},{5,28},{6,14},{7,30},{8,0},{9,16... | collective-permute-start | bytes 3342344 | tf_op jit(solution)/shard_map/ppermute | solution.py:326
  123.8 25.5 %collective-permute-start.28 = (bf16[256,2176]{1,0:T(8,128)(2,1)S(1)}, bf16[256,2176]{1,0:T(8,128)(2,1)}, u32[]{:S(2)}, u32[]{:S(2)}) collective-permute-start(bf16[256,2176]{1,0:T(8,128)(2,1)S(1)} %copy-done.49), channel_id=1, source_target_pairs={{0,0},{1,16},{2,2},{3,18},{4,4},{5,20},{6,6},{7,22},{8,8},{9,24},{... | collective-permute-start | bytes 3342344 | tf_op jit(solution)/shard_map/ppermute | solution.py:326
  136.7 53.0 %collective-permute-start.36 = (bf16[256,2176]{1,0:T(8,128)(2,1)}, bf16[256,2176]{1,0:T(8,128)(2,1)S(1)}, u32[]{:S(2)}, u32[]{:S(2)}) collective-permute-start(bf16[256,2176]{1,0:T(8,128)(2,1)} %collective-permute-done.31), channel_id=1, source_target_pairs={{0,2},{1,0},{2,3},{3,1},{4,6},{5,4},{6,7},{7,5},{8,10},{9,8},{10,1... | collective-permute-start | bytes 3342344 | tf_op jit(solution)/shard_map/ppermute | solution.py:326
  147.8 52.7 %collective-permute-start.20 = (bf16[3,64,1024]{2,1,0:T(8,128)(2,1)S(1)}, bf16[3,64,1024]{2,1,0:T(8,128)(2,1)S(1)}, u32[]{:S(2)}, u32[]{:S(2)}) collective-permute-start(bf16[3,64,1024]{2,1,0:T(8,128)(2,1)S(1)} %get-tuple-element.122), channel_id=1, source_target_pairs={{0,4},{1,5},{2,6},{3,7},{4,0},{5,1},{6,2},{7,3},{8,12},{9,13},{10,... | collective-permute-start | bytes 1179656 | tf_op jit(solution)/shard_map/ppermute | solution.py:326
  149.3 51.3 %collective-permute-start.21 = (bf16[3,64,1024]{2,1,0:T(8,128)(2,1)S(1)}, bf16[3,64,1024]{2,1,0:T(8,128)(2,1)S(1)}, u32[]{:S(2)}, u32[]{:S(2)}) collective-permute-start(bf16[3,64,1024]{2,1,0:T(8,128)(2,1)S(1)} %get-tuple-element.121), channel_id=1, source_target_pairs={{0,2},{1,3},{2,0},{3,1},{4,6},{5,7},{6,4},{7,5},{8,10},{9,11},{10,... | collective-permute-start | bytes 1179656 | tf_op jit(solution)/shard_map/ppermute | solution.py:326
  150.3 50.3 %collective-permute-start.22 = (bf16[3,64,1024]{2,1,0:T(8,128)(2,1)S(1)}, bf16[3,64,1024]{2,1,0:T(8,128)(2,1)S(1)}, u32[]{:S(2)}, u32[]{:S(2)}) collective-permute-start(bf16[3,64,1024]{2,1,0:T(8,128)(2,1)S(1)} %get-tuple-element.120), channel_id=1, source_target_pairs={{0,6},{1,7},{2,4},{3,5},{4,2},{5,3},{6,0},{7,1},{8,14},{9,15},{10,... | collective-permute-start | bytes 1179656 | tf_op jit(solution)/shard_map/ppermute | solution.py:326
  159.7 98.5 %collective-permute-start.37 = (bf16[256,2176]{1,0:T(8,128)(2,1)}, bf16[256,2176]{1,0:T(8,128)(2,1)}, u32[]{:S(2)}, u32[]{:S(2)}) collective-permute-start(bf16[256,2176]{1,0:T(8,128)(2,1)} %collective-permute-done.31), channel_id=1, source_target_pairs={{0,6},{1,4},{2,7},{3,5},{4,2},{5,0},{6,3},{7,1},{8,14},{9,12},{10,... | collective-permute-start | bytes 3342344 | tf_op jit(solution)/shard_map/ppermute | solution.py:326
  190.7 67.6 %collective-permute-start.29 = (bf16[256,2176]{1,0:T(8,128)(2,1)}, bf16[256,2176]{1,0:T(8,128)(2,1)}, u32[]{:S(2)}, u32[]{:S(2)}) collective-permute-start(bf16[256,2176]{1,0:T(8,128)(2,1)} %collective-permute-done.28), channel_id=1, source_target_pairs={{0,0},{1,2},{2,1},{3,3},{4,4},{5,6},{6,5},{7,7},{8,8},{9,10},{10,9... | collective-permute-start | bytes 3342344 | tf_op jit(solution)/shard_map/ppermute | solution.py:326
  200.5 59.5 %collective-permute-start.30 = (bf16[256,2176]{1,0:T(8,128)(2,1)}, bf16[256,2176]{1,0:T(8,128)(2,1)}, u32[]{:S(2)}, u32[]{:S(2)}) collective-permute-start(bf16[256,2176]{1,0:T(8,128)(2,1)} %collective-permute-done.28), channel_id=1, source_target_pairs={{0,4},{1,6},{2,5},{3,7},{4,0},{5,2},{6,1},{7,3},{8,12},{9,14},{10,... | collective-permute-start | bytes 3342344 | tf_op jit(solution)/shard_map/ppermute | solution.py:326
  200.6 61.1 %collective-permute-start.34 = (bf16[256,2176]{1,0:T(8,128)(2,1)}, bf16[256,2176]{1,0:T(8,128)(2,1)}, u32[]{:S(2)}, u32[]{:S(2)}) collective-permute-start(bf16[256,2176]{1,0:T(8,128)(2,1)} %collective-permute-done.28), channel_id=1, source_target_pairs={{0,2},{1,0},{2,3},{3,1},{4,6},{5,4},{6,7},{7,5},{8,10},{9,8},{10,1... | collective-permute-start | bytes 3342344 | tf_op jit(solution)/shard_map/ppermute | solution.py:326
  200.6 68.2 %collective-permute-start.35 = (bf16[256,2176]{1,0:T(8,128)(2,1)}, bf16[256,2176]{1,0:T(8,128)(2,1)}, u32[]{:S(2)}, u32[]{:S(2)}) collective-permute-start(bf16[256,2176]{1,0:T(8,128)(2,1)} %collective-permute-done.28), channel_id=1, source_target_pairs={{0,6},{1,4},{2,7},{3,5},{4,2},{5,0},{6,3},{7,1},{8,14},{9,12},{10,... | collective-permute-start | bytes 3342344 | tf_op jit(solution)/shard_map/ppermute | solution.py:326
  284.1 26.0 %collective-permute-start.56 = (bf16[128,2048]{1,0:T(8,128)(2,1)S(1)}, bf16[128,2048]{1,0:T(8,128)(2,1)S(1)}, u32[]{:S(2)}, u32[]{:S(2)}) collective-permute-start(bf16[128,2048]{1,0:T(8,128)(2,1)S(1)} %get-tuple-element.39), channel_id=1, source_target_pairs={{0,8},{1,9},{2,10},{3,11},{4,12},{5,13},{6,14},{7,15},{8,0},{9,1},... | collective-permute-start | bytes 1572872 | tf_op jit(solution)/shard_map/ppermute | solution.py:326
  290.1 36.6 %collective-permute-start.58 = (bf16[128,2048]{1,0:T(8,128)(2,1)S(1)}, bf16[128,2048]{1,0:T(8,128)(2,1)S(1)}, u32[]{:S(2)}, u32[]{:S(2)}) collective-permute-start(bf16[128,2048]{1,0:T(8,128)(2,1)S(1)} %get-tuple-element.39), channel_id=1, source_target_pairs={{0,24},{1,25},{2,26},{3,27},{4,28},{5,29},{6,30},{7,31},{8,16},{9,... | collective-permute-start | bytes 1572872 | tf_op jit(solution)/shard_map/ppermute | solution.py:326
  294.1 38.1 %collective-permute-start.39 = (bf16[128,2048]{1,0:T(8,128)(2,1)S(1)}, bf16[128,2048]{1,0:T(8,128)(2,1)S(1)}, u32[]{:S(2)}, u32[]{:S(2)}) collective-permute-start(bf16[128,2048]{1,0:T(8,128)(2,1)S(1)} %get-tuple-element.104), channel_id=1, source_target_pairs={{0,8},{1,9},{2,10},{3,11},{4,12},{5,13},{6,14},{7,15},{8,0},{9,1},... | collective-permute-start | bytes 1572872 | tf_op jit(solution)/shard_map/ppermute | solution.py:326
  294.8 75.6 %collective-permute-start.40 = (bf16[128,2048]{1,0:T(8,128)(2,1)S(1)}, bf16[128,2048]{1,0:T(8,128)(2,1)S(1)}, u32[]{:S(2)}, u32[]{:S(2)}) collective-permute-start(bf16[128,2048]{1,0:T(8,128)(2,1)S(1)} %get-tuple-element.106), channel_id=1, source_target_pairs={{0,16},{1,17},{2,18},{3,19},{4,20},{5,21},{6,22},{7,23},{8,24},{9,... | collective-permute-start | bytes 1572872 | tf_op jit(solution)/shard_map/ppermute | solution.py:326
  310.1 60.2 %collective-permute-start.41 = (bf16[128,2048]{1,0:T(8,128)(2,1)S(1)}, bf16[128,2048]{1,0:T(8,128)(2,1)S(1)}, u32[]{:S(2)}, u32[]{:S(2)}) collective-permute-start(bf16[128,2048]{1,0:T(8,128)(2,1)S(1)} %get-tuple-element.105), channel_id=1, source_target_pairs={{0,24},{1,25},{2,26},{3,27},{4,28},{5,29},{6,30},{7,31},{8,16},{9,... | collective-permute-start | bytes 1572872 | tf_op jit(solution)/shard_map/ppermute | solution.py:326
  326.9 94.9 %collective-permute-start.59 = (bf16[512,2048]{1,0:T(8,128)(2,1)S(1)}, bf16[512,2048]{1,0:T(8,128)(2,1)S(1)}, u32[]{:S(2)}, u32[]{:S(2)}) collective-permute-start(bf16[512,2048]{1,0:T(8,128)(2,1)S(1)} %pad_maximum_fusion.4), channel_id=1, source_target_pairs={{0,1},{1,0},{2,3},{3,2},{4,5},{5,4},{6,7},{7,6},{8,9},{9,8},{10,11... | collective-permute-start | bytes 6291464 | tf_op jit(solution)/shard_map/ppermute | solution.py:326
  371.1 34.4 %collective-permute-start.42 = (bf16[128,2048]{1,0:T(8,128)(2,1)S(1)}, bf16[128,2048]{1,0:T(8,128)(2,1)S(1)}, u32[]{:S(2)}, u32[]{:S(2)}) collective-permute-start(bf16[128,2048]{1,0:T(8,128)(2,1)S(1)} %get-tuple-element.41), channel_id=1, source_target_pairs={{0,8},{1,9},{2,10},{3,11},{4,12},{5,13},{6,14},{7,15},{8,0},{9,1},... | collective-permute-start | bytes 1572872 | tf_op jit(solution)/shard_map/ppermute | solution.py:326
  383.1 38.2 %collective-permute-start.43 = (bf16[128,2048]{1,0:T(8,128)(2,1)S(1)}, bf16[128,2048]{1,0:T(8,128)(2,1)S(1)}, u32[]{:S(2)}, u32[]{:S(2)}) collective-permute-start(bf16[128,2048]{1,0:T(8,128)(2,1)S(1)} %get-tuple-element.41), channel_id=1, source_target_pairs={{0,16},{1,17},{2,18},{3,19},{4,20},{5,21},{6,22},{7,23},{8,24},{9,... | collective-permute-start | bytes 1572872 | tf_op jit(solution)/shard_map/ppermute | solution.py:326
  385.1 36.2 %collective-permute-start.44 = (bf16[128,2048]{1,0:T(8,128)(2,1)S(1)}, bf16[128,2048]{1,0:T(8,128)(2,1)S(1)}, u32[]{:S(2)}, u32[]{:S(2)}) collective-permute-start(bf16[128,2048]{1,0:T(8,128)(2,1)S(1)} %get-tuple-element.41), channel_id=1, source_target_pairs={{0,24},{1,25},{2,26},{3,27},{4,28},{5,29},{6,30},{7,31},{8,16},{9,... | collective-permute-start | bytes 1572872 | tf_op jit(solution)/shard_map/ppermute | solution.py:326
  450.9 33.7 %collective-permute-start.61 = (bf16[128,2048]{1,0:T(8,128)(2,1)}, bf16[128,2048]{1,0:T(8,128)(2,1)}, u32[]{:S(2)}, u32[]{:S(2)}) collective-permute-start(bf16[128,2048]{1,0:T(8,128)(2,1)} %get-tuple-element.98), channel_id=1, source_target_pairs={{0,8},{1,9},{2,10},{3,11},{4,12},{5,13},{6,14},{7,15},{8,0},{9,1},... | collective-permute-start | bytes 1572872 | tf_op jit(solution)/shard_map/ppermute | solution.py:326
  460.9 38.5 %collective-permute-start.62 = (bf16[128,2048]{1,0:T(8,128)(2,1)}, bf16[128,2048]{1,0:T(8,128)(2,1)}, u32[]{:S(2)}, u32[]{:S(2)}) collective-permute-start(bf16[128,2048]{1,0:T(8,128)(2,1)} %get-tuple-element.100), channel_id=1, source_target_pairs={{0,16},{1,17},{2,18},{3,19},{4,20},{5,21},{6,22},{7,23},{8,24},{9,... | collective-permute-start | bytes 1572872 | tf_op jit(solution)/shard_map/ppermute | solution.py:326
  462.7 36.7 %collective-permute-start.63 = (bf16[128,2048]{1,0:T(8,128)(2,1)}, bf16[128,2048]{1,0:T(8,128)(2,1)}, u32[]{:S(2)}, u32[]{:S(2)}) collective-permute-start(bf16[128,2048]{1,0:T(8,128)(2,1)} %get-tuple-element.99), channel_id=1, source_target_pairs={{0,24},{1,25},{2,26},{3,27},{4,28},{5,29},{6,30},{7,31},{8,16},{9,... | collective-permute-start | bytes 1572872 | tf_op jit(solution)/shard_map/ppermute | solution.py:326
  468.2 89.7 %collective-permute-start.46 = (bf16[512,2048]{1,0:T(8,128)(2,1)S(1)}, bf16[512,2048]{1,0:T(8,128)(2,1)S(1)}, u32[]{:S(2)}, u32[]{:S(2)}) collective-permute-start(bf16[512,2048]{1,0:T(8,128)(2,1)S(1)} %convolution_convert_fusion.6), channel_id=1, source_target_pairs={{0,1},{1,0},{2,3},{3,2},{4,5},{5,4},{6,7},{7,6},{8,9},{9,8},{10,11... | collective-permute-start | bytes 6291464 | tf_op jit(solution)/shard_map/ppermute | solution.py:326
  502.8 32.3 %collective-permute-start.64 = (bf16[128,2048]{1,0:T(8,128)(2,1)S(1)}, bf16[128,2048]{1,0:T(8,128)(2,1)S(1)}, u32[]{:S(2)}, u32[]{:S(2)}) collective-permute-start(bf16[128,2048]{1,0:T(8,128)(2,1)S(1)} %get-tuple-element.36), channel_id=1, source_target_pairs={{0,8},{1,9},{2,10},{3,11},{4,12},{5,13},{6,14},{7,15},{8,0},{9,1},... | collective-permute-start | bytes 1572872 | tf_op jit(solution)/shard_map/ppermute | solution.py:326
  513.5 38.2 %collective-permute-start.65 = (bf16[128,2048]{1,0:T(8,128)(2,1)S(1)}, bf16[128,2048]{1,0:T(8,128)(2,1)S(1)}, u32[]{:S(2)}, u32[]{:S(2)}) collective-permute-start(bf16[128,2048]{1,0:T(8,128)(2,1)S(1)} %get-tuple-element.36), channel_id=1, source_target_pairs={{0,16},{1,17},{2,18},{3,19},{4,20},{5,21},{6,22},{7,23},{8,24},{9,... | collective-permute-start | bytes 1572872 | tf_op jit(solution)/shard_map/ppermute | solution.py:326
  515.3 36.4 %collective-permute-start.66 = (bf16[128,2048]{1,0:T(8,128)(2,1)S(1)}, bf16[128,2048]{1,0:T(8,128)(2,1)S(1)}, u32[]{:S(2)}, u32[]{:S(2)}) collective-permute-start(bf16[128,2048]{1,0:T(8,128)(2,1)S(1)} %get-tuple-element.36), channel_id=1, source_target_pairs={{0,24},{1,25},{2,26},{3,27},{4,28},{5,29},{6,30},{7,31},{8,16},{9,... | collective-permute-start | bytes 1572872 | tf_op jit(solution)/shard_map/ppermute | solution.py:326
  662.8 82.0 %collective-permute-start.96 = (bf16[256,2176]{1,0:T(8,128)(2,1)S(1)}, bf16[256,2176]{1,0:T(8,128)(2,1)S(1)}, u32[]{:S(2)}, u32[]{:S(2)}) collective-permute-start(bf16[256,2176]{1,0:T(8,128)(2,1)S(1)} %copy-done.48), channel_id=1, source_target_pairs={{0,0},{1,2},{2,1},{3,3},{4,4},{5,6},{6,5},{7,7},{8,8},{9,10},{10,9... | collective-permute-start | bytes 3342344 | tf_op jit(solution)/shard_map/ppermute | solution.py:326
  671.9 74.3 %collective-permute-start.97 = (bf16[256,2176]{1,0:T(8,128)(2,1)S(1)}, bf16[256,2176]{1,0:T(8,128)(2,1)S(1)}, u32[]{:S(2)}, u32[]{:S(2)}) collective-permute-start(bf16[256,2176]{1,0:T(8,128)(2,1)S(1)} %pad_maximum_fusion.13), channel_id=1, source_target_pairs={{0,4},{1,6},{2,5},{3,7},{4,0},{5,2},{6,1},{7,3},{8,12},{9,14},{10,... | collective-permute-start | bytes 3342344 | tf_op jit(solution)/shard_map/ppermute | solution.py:326
  677.0 72.5 %collective-permute-start.98 = (bf16[256,2176]{1,0:T(8,128)(2,1)S(1)}, bf16[256,2176]{1,0:T(8,128)(2,1)S(1)}, u32[]{:S(2)}, u32[]{:S(2)}) collective-permute-start(bf16[256,2176]{1,0:T(8,128)(2,1)S(1)} %pad_maximum_fusion.14), channel_id=1, source_target_pairs={{0,1},{1,3},{2,0},{3,2},{4,5},{5,7},{6,4},{7,6},{8,9},{9,11},{10,8... | collective-permute-start | bytes 3342344 | tf_op jit(solution)/shard_map/ppermute | solution.py:326
  677.0 47.7 %collective-permute-start.93 = (bf16[256,768]{1,0:T(8,128)(2,1)S(1)}, bf16[256,768]{1,0:T(8,128)(2,1)S(1)}, u32[]{:S(2)}, u32[]{:S(2)}) collective-permute-start(bf16[256,768]{1,0:T(8,128)(2,1)S(1)} %get-tuple-element.77), channel_id=1, source_target_pairs={{0,1},{1,3},{2,0},{3,2},{4,5},{5,7},{6,4},{7,6},{8,9},{9,11},{10,8... | collective-permute-start | bytes 1179656 | tf_op jit(solution)/shard_map/ppermute | solution.py:326
  680.6 70.9 %collective-permute-start.99 = (bf16[256,2176]{1,0:T(8,128)(2,1)S(1)}, bf16[256,2176]{1,0:T(8,128)(2,1)S(1)}, u32[]{:S(2)}, u32[]{:S(2)}) collective-permute-start(bf16[256,2176]{1,0:T(8,128)(2,1)S(1)} %pad_maximum_fusion.15), channel_id=1, source_target_pairs={{0,5},{1,7},{2,4},{3,6},{4,1},{5,3},{6,0},{7,2},{8,13},{9,15},{10,... | collective-permute-start | bytes 3342344 | tf_op jit(solution)/shard_map/ppermute | solution.py:326
  746.2 40.4 %collective-permute-start.103 = (bf16[256,2176]{1,0:T(8,128)(2,1)S(1)}, bf16[256,2176]{1,0:T(8,128)(2,1)S(1)}, u32[]{:S(2)}, u32[]{:S(2)}) collective-permute-start(bf16[256,2176]{1,0:T(8,128)(2,1)S(1)} %pad_maximum_fusion.18), channel_id=1, source_target_pairs={{0,1},{1,3},{2,0},{3,2},{4,5},{5,7},{6,4},{7,6},{8,9},{9,11},{10,8... | collective-permute-start | bytes 3342344 | tf_op jit(solution)/shard_map/ppermute | solution.py:326
  749.5 49.1 %collective-permute-start.104 = (bf16[256,2176]{1,0:T(8,128)(2,1)S(1)}, bf16[256,2176]{1,0:T(8,128)(2,1)S(1)}, u32[]{:S(2)}, u32[]{:S(2)}) collective-permute-start(bf16[256,2176]{1,0:T(8,128)(2,1)S(1)} %pad_maximum_fusion.19), channel_id=1, source_target_pairs={{0,5},{1,7},{2,4},{3,6},{4,1},{5,3},{6,0},{7,2},{8,13},{9,15},{10,... | collective-permute-start | bytes 3342344 | tf_op jit(solution)/shard_map/ppermute | solution.py:326
  751.5 111.1 %collective-permute-start.74 = (bf16[512,2048]{1,0:T(8,128)(2,1)}, bf16[512,2048]{1,0:T(8,128)(2,1)}, u32[]{:S(2)}, u32[]{:S(2)}) collective-permute-start(bf16[512,2048]{1,0:T(8,128)(2,1)} %convolution_convert_fusion.4), channel_id=1, source_target_pairs={{0,1},{1,0},{2,3},{3,2},{4,5},{5,4},{6,7},{7,6},{8,9},{9,8},{10,11... | collective-permute-start | bytes 6291464 | tf_op jit(solution)/shard_map/ppermute | solution.py:326
  753.6 57.8 %collective-permute-start.90 = (bf16[256,768]{1,0:T(8,128)(2,1)}, bf16[256,768]{1,0:T(8,128)(2,1)}, u32[]{:S(2)}, u32[]{:S(2)}) collective-permute-start(bf16[256,768]{1,0:T(8,128)(2,1)} %add_convert_fusion.3), channel_id=1, source_target_pairs={{0,0},{1,16},{2,2},{3,18},{4,4},{5,20},{6,6},{7,22},{8,8},{9,24},{... | collective-permute-start | bytes 1179656 | tf_op jit(solution)/shard_map/ppermute | solution.py:326
  760.4 52.2 %collective-permute-start.95 = (bf16[256,768]{1,0:T(8,128)(2,1)}, bf16[256,768]{1,0:T(8,128)(2,1)}, u32[]{:S(2)}, u32[]{:S(2)}) collective-permute-start(bf16[256,768]{1,0:T(8,128)(2,1)} %add_convert_fusion.2), channel_id=1, source_target_pairs={{0,8},{1,24},{2,10},{3,26},{4,12},{5,28},{6,14},{7,30},{8,0},{9,16... | collective-permute-start | bytes 1179656 | tf_op jit(solution)/shard_map/ppermute | solution.py:326
  786.6 31.6 %collective-permute-start.100 = (bf16[256,2176]{1,0:T(8,128)(2,1)}, bf16[256,2176]{1,0:T(8,128)(2,1)}, u32[]{:S(2)}, u32[]{:S(2)}) collective-permute-start(bf16[256,2176]{1,0:T(8,128)(2,1)} %add_convert_fusion.1), channel_id=1, source_target_pairs={{0,0},{1,16},{2,2},{3,18},{4,4},{5,20},{6,6},{7,22},{8,8},{9,24},{... | collective-permute-start | bytes 3342344 | tf_op jit(solution)/shard_map/ppermute | solution.py:326
  800.2 58.4 %collective-permute-start.105 = (bf16[256,2176]{1,0:T(8,128)(2,1)}, bf16[256,2176]{1,0:T(8,128)(2,1)}, u32[]{:S(2)}, u32[]{:S(2)}) collective-permute-start(bf16[256,2176]{1,0:T(8,128)(2,1)} %add_convert_fusion), channel_id=1, source_target_pairs={{0,8},{1,24},{2,10},{3,26},{4,12},{5,28},{6,14},{7,30},{8,0},{9,16... | collective-permute-start | bytes 3342344 | tf_op jit(solution)/shard_map/ppermute | solution.py:326
  811.5 132.0 %collective-permute-start.47 = (bf16[128,2048]{1,0:T(8,128)(2,1)}, bf16[128,2048]{1,0:T(8,128)(2,1)}, u32[]{:S(2)}, u32[]{:S(2)}) collective-permute-start(bf16[128,2048]{1,0:T(8,128)(2,1)} %get-tuple-element.101), channel_id=1, source_target_pairs={{0,8},{1,9},{2,10},{3,11},{4,12},{5,13},{6,14},{7,15},{8,0},{9,1},... | collective-permute-start | bytes 1572872 | tf_op jit(solution)/shard_map/ppermute | solution.py:326
  812.6 130.8 %collective-permute-start.48 = (bf16[128,2048]{1,0:T(8,128)(2,1)}, bf16[128,2048]{1,0:T(8,128)(2,1)}, u32[]{:S(2)}, u32[]{:S(2)}) collective-permute-start(bf16[128,2048]{1,0:T(8,128)(2,1)} %get-tuple-element.103), channel_id=1, source_target_pairs={{0,16},{1,17},{2,18},{3,19},{4,20},{5,21},{6,22},{7,23},{8,24},{9,... | collective-permute-start | bytes 1572872 | tf_op jit(solution)/shard_map/ppermute | solution.py:326
  866.3 49.8 %collective-permute-start.76 = (bf16[128,2048]{1,0:T(8,128)(2,1)S(1)}, bf16[128,2048]{1,0:T(8,128)(2,1)S(1)}, u32[]{:S(2)}, u32[]{:S(2)}) collective-permute-start(bf16[128,2048]{1,0:T(8,128)(2,1)S(1)} %get-tuple-element.97), channel_id=1, source_target_pairs={{0,16},{1,17},{2,18},{3,19},{4,20},{5,21},{6,22},{7,23},{8,24},{9,... | collective-permute-start | bytes 1572872 | tf_op jit(solution)/shard_map/ppermute | solution.py:326
  871.9 44.2 %collective-permute-start.77 = (bf16[128,2048]{1,0:T(8,128)(2,1)S(1)}, bf16[128,2048]{1,0:T(8,128)(2,1)S(1)}, u32[]{:S(2)}, u32[]{:S(2)}) collective-permute-start(bf16[128,2048]{1,0:T(8,128)(2,1)S(1)} %get-tuple-element.96), channel_id=1, source_target_pairs={{0,24},{1,25},{2,26},{3,27},{4,28},{5,29},{6,30},{7,31},{8,16},{9,... | collective-permute-start | bytes 1572872 | tf_op jit(solution)/shard_map/ppermute | solution.py:326
  884.3 59.1 %collective-permute-start.49 = (bf16[128,2048]{1,0:T(8,128)(2,1)}, bf16[128,2048]{1,0:T(8,128)(2,1)}, u32[]{:S(2)}, u32[]{:S(2)}) collective-permute-start(bf16[128,2048]{1,0:T(8,128)(2,1)} %get-tuple-element.102), channel_id=1, source_target_pairs={{0,24},{1,25},{2,26},{3,27},{4,28},{5,29},{6,30},{7,31},{8,16},{9,... | collective-permute-start | bytes 1572872 | tf_op jit(solution)/shard_map/ppermute | solution.py:326
  (150 other events, 2538.3 us)
